TPU v7x, 256 devices: a whole 4x4x8 slice. The times are simulated.
256 devices in a mesh: doc: 8 (over x, core), term: 32 (over y, z).
Axes of the slice: x: 4, y: 4, z: 8, core: 2. Of those that a mesh axis runs over, the one named last changes fastest.
Arguments:
- counts: int32 [3072, 262144], P('doc', 'term'), may hold values from 0 to 7
- doc_freq: int32 [262144], P('term'), may hold values from 1 to 2097151, as said below
- sketch_seed: int32 [1], replicated, may hold values from 0 to 1048575
Outputs:
- ortho_basis: float32 [3072, 256], P('doc')
- projected_panel: bfloat16 [256, 262144], P('doc', 'term')
- column_mean: float32 [262144], P('term')
Inputs may be any that keep to these rules, and one draw needn't show every extreme that they name: `doc_freq`: document frequencies spread evenly in their logarithm.
All inputs are finite; a program needn't handle non-finite values.
Results may differ from a plain program's by a relative error of at most 0.018.
Values may be sent and summed in bfloat16 or wider, within the bound.
No kernel may reach another device: no remote copies, remote signals or barrier semaphores. Data moves between devices by JAX's collectives and lax.ppermute only.
A program may use at most 64 MiB of HBM per device.

v0:
```python
import jax
import jax.numpy as jnp
from jax import lax
from jax.sharding import PartitionSpec as P

TERMS = 262144
SKETCH = 256
CORPUS = 2000000000


byte_sum_std = 147.8


def sketch_tile(seed_value, first_term, row_count, col_count):
    term_ids = first_term + lax.iota(jnp.int32, row_count)
    columns = lax.iota(jnp.int32, col_count)
    hashed = term_ids[:, None] * col_count + columns[None, :]
    hashed = hashed ^ seed_value * 668265263
    hashed = hashed * 1640531527
    hashed = hashed ^ lax.shift_right_logical(hashed, jnp.int32(15))
    hashed = hashed * 739982445
    hashed = hashed ^ lax.shift_right_logical(hashed, jnp.int32(13))
    summed = (hashed & 255) + (lax.shift_right_logical(hashed, jnp.int32(8)) & 255)
    summed = summed + (lax.shift_right_logical(hashed, jnp.int32(16)) & 255)
    summed = summed + (lax.shift_right_logical(hashed, jnp.int32(24)) & 255)
    factor = 1.0 / (byte_sum_std * TERMS**0.5)
    return ((summed - 510).astype(jnp.float32) * factor).astype(jnp.bfloat16)


def tfidf_tile(counts_tile, df_tile):
    counted = jnp.maximum(counts_tile.astype(jnp.float32), 1.0)
    term_freq = jnp.where(counts_tile > 0, 1.0 + jnp.log(counted), 0.0)
    inverse = 1.0 + jnp.log(jnp.float32(CORPUS) / df_tile.astype(jnp.float32))
    return term_freq * inverse[None, :]


def gram_of(matrix):
    return jnp.dot(
        matrix.T, matrix, precision=lax.Precision.HIGHEST, preferred_element_type=jnp.float32
    )


def solve_rows(lower_factor, sketch_rows):
    return lax.linalg.triangular_solve(lower_factor, sketch_rows.T, left_side=True, lower=True).T


def body(counts, doc_freq, sketch_seed):
    tile_cols = counts.shape[1]
    first_term = lax.axis_index("term") * tile_cols
    tfidf = tfidf_tile(counts, doc_freq)
    column_total = lax.psum(jnp.sum(tfidf, axis=0), "doc")
    column_mean = column_total / jnp.float32(counts.shape[0] * lax.axis_size("doc"))
    weighted = (tfidf - column_mean[None, :]).astype(jnp.bfloat16)
    test_matrix = sketch_tile(sketch_seed[0], first_term, tile_cols, SKETCH)
    partial_value = jnp.dot(weighted, test_matrix, preferred_element_type=jnp.float32)
    sketch = lax.psum(partial_value, "term")
    gram_matrix = lax.psum(gram_of(sketch), "doc")
    lower_factor = jnp.linalg.cholesky(gram_matrix)
    ortho_basis = solve_rows(lower_factor, sketch)
    basis_left = ortho_basis.astype(jnp.bfloat16).T
    projected = lax.psum_scatter(
        jnp.dot(basis_left, weighted, preferred_element_type=jnp.float32).astype(jnp.bfloat16),
        "doc",
        scatter_dimension=0,
        tiled=True,
    )
    return (ortho_basis, projected, column_mean)


def solution(mesh):
    placed = (P("doc", "term"), P("term"), P())
    return jax.shard_map(
        body,
        mesh=mesh,
        in_specs=placed,
        out_specs=(P("doc", None), P("doc", "term"), P("term")),
        check_vma=False,
    )
```

profile of v0, /device:TPU:1, one launch (start us, length us, event | category | flops | bytes accessed | tf_op | source)
XLA Modules:
  0.0 394.4 jit_solution(4613536054819183466)
XLA Ops:
  7.9 0.8 log_add_fusion
  8.7 11.8 %fusion.1 = f32[8192]{0:T(1024)S(1)} fusion(s32[384,8192]{1,0:T(8,128)} %param.3, f32[8192]{0:T(1024)S(1)} %log_add_fusion), kind=kLoop, calls=%fused_computation.9 | loop fusion | flops 22011904 | bytes 12648448 | tf_op jit(solution)/shard_map/reduce_sum | solution.py:51
  20.4 23.6 %psum.21 = f32[8192]{0:T(1024)S(1)} all-reduce(f32[8192]{0:T(1024)S(1)} %fusion.1), channel_id=1, replica_groups=mesh['doc'=8,'term'=32] {'doc'}, use_global_device_ids=true, to_apply=%region_1.2 | all-reduce | flops 8192 | bytes 65536 | tf_op jit(solution)/shard_map/psum | solution.py:51
  44.0 15.5 %fusion.2 = f32[384,256]{1,0:T(8,128)} fusion(s32[]{:T(128)} %bitcast, s32[8192]{0:T(1024)S(1)} %add_multiply_fusion, s32[384,8192]{1,0:T(8,128)} %param.3, f32[8192]{0:T(1024)S(1)} %broadcast_multiply_fusion, f32[8192]{0:T(1024)S(1)} %log_add_fusion), kind=kOutput, calls=%fused_computation.10 | convolution fusion | flops 1681915904 | bytes 13074436 | tf_op jit(solution)/shard_map/dot_general | solution.py:55
  59.7 144.4 %all-reduce.4.cloned.1.call-done = f32[384,256]{1,0:T(8,128)} async-done(((f32[384,256]{1,0:T(8,128)}), f32[384,256]{1,0:T(8,128)}) %all-reduce.4.cloned.1.call-update) | async-done | bytes 393232 | tf_op jit(solution)/shard_map/psum | solution.py:56
  204.0 2.7 fusion.35
  207.0 64.8 %all-reduce.6.cloned.1.call-done = f32[256,256]{0,1:T(8,128)} async-done(((f32[256,256]{0,1:T(8,128)}), f32[256,256]{0,1:T(8,128)}) %all-reduce.6.cloned.1.call-update) | async-done | bytes 262160 | tf_op jit(solution)/shard_map/psum | solution.py:57
  271.8 1.1 copy.7
  272.9 1.0 fusion.15
  273.9 11.7 %cholesky.50 = f32[128,128]{1,0:T(8,128)S(1)} custom-call(f32[128,128]{1,0:T(8,128)S(1)} %cholesky.118), custom_call_target="Cholesky" | custom-call | tf_op jit(solution)/shard_map/jit(cholesky)/cholesky | solution.py:58
  285.6 9.8 %custom-call.14 = f32[1,128,128]{1,2,0:T(8,128)S(1)} custom-call(f32[1,128,128]{2,1,0:T(8,128)S(1)} %get-tuple-element.27), custom_call_target="InvertDiagBlocksLowerTriangular" | custom-call | tf_op jit(solution)/shard_map/jit(cholesky)/cholesky | solution.py:58
  296.0 11.7 %cholesky.105 = f32[128,128]{1,0:T(8,128)S(1)} custom-call(f32[128,128]{1,0:T(8,128)S(1)} %convolution_subtract_fusion.1), custom_call_target="Cholesky" | custom-call | tf_op jit(solution)/shard_map/jit(cholesky)/cholesky | solution.py:58
  307.7 0.7 compare_reduce_fusion
  309.8 4.1 %while.1 = (s32[]{:T(128)}, f32[256,256]{1,0:T(8,128)S(1)}, s32[2,2]{1,0:T(2,128)S(1)}, f32[2,128,128]{2,1,0:T(8,128)S(1)}, s32[]{:T(128)}) while((s32[]{:T(128)}, f32[256,256]{1,0:T(8,128)S(1)}, s32[2,2]{1,0:T(2,128)S(1)}, f32[2,128,128]{2,1,0:T(8,128)S(1)}, s32[]{:T(128)}) %tuple.28), condition=%wide.while_cond, body=%wide.while_body.sunk | while | flops 2 | bytes 131189 | solution.py:44
  310.0 0.6 fusion.43
  310.6 1.4 bitcast_dynamic-update-slice_fusion.2
  312.0 0.6 fusion.43
  312.6 1.4 bitcast_dynamic-update-slice_fusion.2
  313.9 19.7 %custom-call.15 = f32[2,128,128]{1,2,0:T(8,128)S(1)} custom-call(f32[2,128,128]{2,1,0:T(8,128)S(1)} %get-tuple-element.10), custom_call_target="InvertDiagBlocksLowerTriangular" | custom-call | tf_op jit(solution)/shard_map/triangular_solve | solution.py:44
  333.6 1.3 fusion.16
  334.9 1.4 convolution_subtract_fusion
  336.8 12.2 %convolution_convert_fusion = bf16[256,8192]{1,0:T(8,128)(2,1)} fusion(f32[128,384]{1,0:T(8,128)S(1)} %fusion.20, f32[128,384]{1,0:T(8,128)S(1)} %fusion.16, s32[384,8192]{1,0:T(8,128)} %param.3, f32[8192]{0:T(1024)S(1)} %broadcast_multiply_fusion, f32[8192]{0:T(1024)S(1)} %log_add_fusion), kind=kOutput, calls=%fused_computation.6 | convolution fusion | flops 1638268928 | bytes 17235968 | tf_op jit(solution)/shard_map/dot_general | solution.py:62
  349.1 0.9 copy.8
  350.0 37.9 %reduce-scatter.2.cloned.1.call-done = bf16[32,8192]{1,0:T(8,128)(2,1)} async-done(((bf16[256,8192]{1,0:T(8,128)(2,1)}), bf16[32,8192]{1,0:T(8,128)(2,1)}) %reduce-scatter.2.cloned.1.call-update) | async-done | bytes 524304 | tf_op jit(solution)/shard_map/reduce_scatter | solution.py:61
  (24 shorter events, 1.5 us)
Async XLA Ops:
  7.2 196.9 %all-reduce.4.cloned.1.call-start = ((), (), s32[]{:S(2)}) async-start(), calls=%async_computation.1 | async-start | bytes 786432 | tf_op jit(solution)/shard_map/psum | solution.py:56
  44.0 292.8 %copy-start = (f32[8192]{0:T(1024)}, f32[8192]{0:T(1024)S(1)}, u32[]{:S(2)}) copy-start(f32[8192]{0:T(1024)S(1)} %broadcast_multiply_fusion) | copy-start | bytes 98308
  59.6 212.2 %all-reduce.6.cloned.1.call-start = ((), (), s32[]{:S(2)}) async-start(), calls=%async_computation.2 | async-start | bytes 524288 | tf_op jit(solution)/shard_map/psum | solution.py:57
  206.7 181.2 %reduce-scatter.2.cloned.1.call-start = ((), (), s32[]{:S(2)}) async-start(), calls=%async_computation.3 | async-start | bytes 4718592 | tf_op jit(solution)/shard_map/reduce_scatter | solution.py:61
Sparse Core Ops, SparseCore 0:
  59.7 144.2 all-reduce.3
  207.0 64.7 all-reduce.5
  349.1 38.6 reduce-scatter.1
where the time goes:
time: 397 us; the launch traced here: 394 us
  waiting for transfers between devices  247 us (62%)
  other arithmetic  67.3 us (17%)
  matrix products  34 us (9%)
  blocking collectives  23.6 us (6%)
  between operations  15.8 us (4%)
  local copies, waits for them, and re-layouts  6 us (2%)
    psum x1, waiting for transfers between devices, body(): sketch = lax.psum(partial_value, 'term')  144 us
    psum x1, waiting for transfers between devices, body(): gram_matrix = lax.psum(gram_of(sketch), 'doc')  64.8 us
    reduce_scatter x1, waiting for transfers between devices, body(): lax.psum_scatter(jnp.dot(basis_left, weighted, preferred_element_type=jnp...  37.9 us
    another operation x6, other arithmetic, body(): lower_factor = jnp.linalg.cholesky(gram_matrix)  34 us
    psum x1, blocking collectives, body(): column_total = lax.psum(jnp.sum(tfidf, axis=0), 'doc')  23.6 us
    another operation x3, other arithmetic, solve_rows(): lax.linalg.triangular_solve(lower_factor, sketch_rows.T, left_side=True,...  19.7 us
    dot_general x1, matrix products, body(): jnp.dot(weighted, test_matrix, preferred_element_type=jnp.float32)  15.5 us
    dot_general x1, matrix products, body(): jnp.dot(basis_left, weighted, preferred_element_type=jnp.float32)  12.2 us
  transfers between devices with their start and end apart: 3, of which 3 were waited for; matrix products, arithmetic and copies ran while one was open for 0% of the time, Pallas kernels for 0%

commit v1 on v0

v1 whole, which is shorter than its diff:
```python
import math

import jax
import jax.numpy as jnp
import numpy as np
from jax import lax
from jax.experimental import pallas as pl
from jax.experimental.pallas import tpu as pltpu
from jax.sharding import Mesh
from jax.sharding import PartitionSpec as P

TERMS = 262144
SKETCH = 256
CORPUS = 2000000000
BYTE_SUM_STD = 147.8
FACTOR = 1.0 / (BYTE_SUM_STD * TERMS**0.5)
HIGHEST = lax.Precision.HIGHEST
F32, BF16, I32 = jnp.float32, jnp.bfloat16, jnp.int32
VMEM_LIMIT = 48 * 1024 * 1024
LANES = 128
PIVOTS = 16
TAIL = 16


def log_count(counts):
    return jnp.log(jnp.maximum(counts.astype(F32), math.exp(-1.0)))


def idf_of(doc_freq):
    return 1.0 + jnp.log(jnp.float32(CORPUS) / doc_freq.astype(F32))


def three_parts(value):
    high = value.astype(BF16)
    rest = value - high.astype(F32)
    middle = rest.astype(BF16)
    low = (rest - middle.astype(F32)).astype(BF16)
    return high, middle, low


def parts_tile(value, rows, shape):
    high, middle, low = (part.astype(F32) for part in three_parts(value))
    where = lax.broadcasted_iota(I32, shape, 0)
    tile = jnp.where(where == 0, high, jnp.where(where == 1, middle, jnp.where(where == 2, low, 0.0)))
    return tile.astype(BF16)


def sketch_kernel(scal_ref, counts_ref, df_ref, s_ref, w_ref, lsum_ref, acc, om):
    step, steps = pl.program_id(0), pl.num_programs(0)
    rows, cols = counts_ref.shape
    first = scal_ref[1] + step * cols
    key = scal_ref[0] * 668265263
    idf = idf_of(df_ref[...])

    @pl.when(step == 0)
    def _():
        acc[...] = jnp.zeros_like(acc)

    for tile in range(cols // LANES):
        at = slice(tile * LANES, (tile + 1) * LANES)
        logs = log_count(counts_ref[:, at])
        total = jnp.sum(logs, axis=0, keepdims=True)
        mean = total * (1.0 / rows)
        lsum_ref[tile : tile + 1, :] = total
        w_ref[:rows, at] = ((logs - mean) * idf[:, at]).astype(BF16)
        w_ref[rows:, at] = parts_tile(idf[:, at] * (1.0 + mean), TAIL, (TAIL, LANES))

    lane = lax.broadcasted_iota(I32, (1, LANES), 1)
    low_key, high_key = key & 255, key & -256
    group = 64
    local = lax.broadcasted_iota(I32, (group, LANES), 0)
    for g in range(cols // group):
        terms = (local + (first + g * group)) * SKETCH
        row_part = (terms ^ high_key) * 1640531527
        for half in range(SKETCH // LANES):
            col_part = ((lane + half * LANES) ^ low_key) * 1640531527
            h = row_part + col_part
            h = h ^ lax.shift_right_logical(h, jnp.int32(15))
            h = h * 739982445
            h = h ^ lax.shift_right_logical(h, jnp.int32(13))
            pair = (h & 0x00FF00FF) + (lax.shift_right_logical(h, jnp.int32(8)) & 0x00FF00FF)
            byte_sum = (pair & 0xFFFF) + lax.shift_right_logical(pair, jnp.int32(16))
            value = (byte_sum - 510).astype(F32) * FACTOR
            om[g * group : (g + 1) * group, half * LANES : (half + 1) * LANES] = value.astype(BF16)

    acc[...] += jnp.dot(w_ref[...], om[...], preferred_element_type=F32)

    @pl.when(step == steps - 1)
    def _():
        shift = jnp.sum(acc[rows:, :], axis=0, keepdims=True)
        for half in range(SKETCH // LANES):
            at = slice(half * LANES, (half + 1) * LANES)
            s_ref[half * rows : (half + 1) * rows, :] = acc[:rows, at] + shift[:, at]


def sketch_call(scalars, counts, doc_freq):
    rows, cols = counts.shape
    block = 1024
    return pl.pallas_call(
        sketch_kernel,
        grid=(cols // block,),
        in_specs=[
            pl.BlockSpec(memory_space=pltpu.SMEM),
            pl.BlockSpec((rows, block), lambda i: (0, i)),
            pl.BlockSpec((1, block), lambda i: (0, i)),
        ],
        out_specs=[
            pl.BlockSpec((2 * rows, LANES), lambda i: (0, 0)),
            pl.BlockSpec((rows + TAIL, block), lambda i: (0, i)),
            pl.BlockSpec((block // LANES, LANES), lambda i: (i, 0)),
        ],
        out_shape=[
            jax.ShapeDtypeStruct((2 * rows, LANES), F32),
            jax.ShapeDtypeStruct((rows + TAIL, cols), BF16),
            jax.ShapeDtypeStruct((cols // LANES, LANES), F32),
        ],
        scratch_shapes=[pltpu.VMEM((rows + TAIL, SKETCH), F32), pltpu.VMEM((block, SKETCH), BF16)],
        compiler_params=pltpu.CompilerParams(vmem_limit_bytes=VMEM_LIMIT),
        name="sketch",
    )(scalars, counts, doc_freq.reshape(1, cols))


def gram_kernel(scal_ref, g_ref, gram_ref, own_ref, full):
    parts, held, _ = g_ref.shape
    half_parts = parts // 2
    held -= TAIL
    docs = 4
    chunk = held // docs
    rows = chunk * half_parts
    for t in range(half_parts):
        for half in range(2):
            block = g_ref[t + half_parts * half].astype(F32)
            mean = block[held : held + 1] + block[held + 1 : held + 2] + block[held + 2 : held + 3]
            value = block[:held] + mean
            at = slice(half * LANES, (half + 1) * LANES)
            for x in range(docs):
                full[x * rows + chunk * t : x * rows + chunk * (t + 1), at] = value[chunk * x : chunk * (x + 1)]
    mean = jnp.sum(full[...], axis=0, keepdims=True) * (1.0 / (docs * rows))
    centred = full[...] - mean
    full[...] = centred
    gram_ref[:SKETCH, :] = lax.dot_general(
        centred, centred, (((0,), (0,)), ((), ())), precision=HIGHEST, preferred_element_type=F32
    )
    row = lax.broadcasted_iota(I32, (8, SKETCH), 0)
    gram_ref[SKETCH:, :] = jnp.where(row == 0, mean, 0.0)
    own_ref[...] = full[pl.ds(pl.multiple_of(scal_ref[0] * rows, 8), rows), :]


def gram_call(scalars, gathered, rows):
    return pl.pallas_call(
        gram_kernel,
        in_specs=[pl.BlockSpec(memory_space=pltpu.SMEM), pl.BlockSpec(memory_space=pltpu.VMEM)],
        out_specs=[pl.BlockSpec(memory_space=pltpu.VMEM)] * 2,
        out_shape=[
            jax.ShapeDtypeStruct((SKETCH + 8, SKETCH), F32),
            jax.ShapeDtypeStruct((rows, SKETCH), F32),
        ],
        scratch_shapes=[pltpu.VMEM((4 * rows, SKETCH), F32)],
        compiler_params=pltpu.CompilerParams(vmem_limit_bytes=VMEM_LIMIT),
        name="gram",
    )(scalars, gathered)


def basis_kernel(scal_ref, mine_ref, theirs_ref, own_ref, q_ref, bt_ref, work):
    my_x, my_core = scal_ref[0], scal_ref[1]
    size = SKETCH
    apart = mine_ref[size:, :] - theirs_ref[size:, :]
    docs = 4 * own_ref.shape[0]
    shift = lax.dot_general(apart, apart, (((0,), (0,)), ((), ())), precision=HIGHEST, preferred_element_type=F32)
    work[...] = (mine_ref[:size, :] + theirs_ref[:size, :]) + (0.5 * docs) * shift

    lane = lax.broadcasted_iota(I32, (PIVOTS, LANES), 1)
    sub = lax.broadcasted_iota(I32, (PIVOTS, LANES), 0)
    for block in range(size // PIVOTS):
        start = block * PIVOTS
        panel = work[start : start + PIVOTS, :]
        spread = [jnp.broadcast_to(panel[:, start + k : start + k + 1], (PIVOTS, LANES)) for k in range(PIVOTS)]
        halves = []
        for half in range(size // LANES):
            piece = panel[:, half * LANES : (half + 1) * LANES]
            local = lane - (start - half * LANES)
            if start // LANES == half:
                piece = jnp.where((local >= 0) & (local < PIVOTS), jnp.where(local == sub, 1.0, 0.0), piece)
            halves.append(piece)
        pivots = jnp.zeros((PIVOTS, LANES), F32)
        for j in range(PIVOTS):
            pivot = jnp.broadcast_to(spread[j][j : j + 1, :], (PIVOTS, LANES))
            pivots = jnp.where(sub == j, pivot, pivots)
            if j + 1 < PIVOTS:
                scale = jnp.where(sub > j, spread[j] * (1.0 / pivot), 0.0)
                for k in range(j + 1, PIVOTS):
                    spread[k] = spread[k] - scale * spread[k][j : j + 1, :]
                halves = [piece - scale * piece[j : j + 1, :] for piece in halves]
        root = lax.rsqrt(pivots)
        factor_rows = jnp.concatenate([piece * root for piece in halves], axis=1)
        work[start : start + PIVOTS, :] = factor_rows
        rest = start + PIVOTS
        if rest < size:
            update = lax.dot_general(
                factor_rows, factor_rows, (((0,), (0,)), ((), ())), precision=HIGHEST, preferred_element_type=F32
            )
            old = work[rest:, :]
            column = lax.broadcasted_iota(I32, old.shape, 1)
            old = jnp.where((column >= start) & (column < rest), 0.0, old)
            work[rest:, :] = old - update[rest:, :]

    row = lax.broadcasted_iota(I32, (size, size), 0)
    column = lax.broadcasted_iota(I32, (size, size), 1)
    inverse = jnp.where(column <= row, work[...], 0.0)
    own = own_ref[...] + 0.5 * apart[0:1, :]
    contract = (((1,), (1,)), ((), ()))
    q_ref[...] = lax.dot_general(own, inverse, contract, precision=HIGHEST, preferred_element_type=F32)
    flipped = lax.dot_general(inverse, own, contract, precision=HIGHEST, preferred_element_type=F32).astype(BF16)
    rows = size // 8
    for x in range(4):
        for core in range(2):
            piece = flipped[rows * (2 * x + core) : rows * (2 * x + core + 1)]
            bt_ref[(my_core + core) & 1, (x - my_x) & 3] = piece


def basis_call(scalars, mine, theirs, own):
    rows = own.shape[0]
    return pl.pallas_call(
        basis_kernel,
        in_specs=[pl.BlockSpec(memory_space=pltpu.SMEM)] + [pl.BlockSpec(memory_space=pltpu.VMEM)] * 3,
        out_specs=[pl.BlockSpec(memory_space=pltpu.VMEM)] * 2,
        out_shape=[
            jax.ShapeDtypeStruct((rows, SKETCH), F32),
            jax.ShapeDtypeStruct((2, 4, SKETCH // 8, rows), BF16),
        ],
        scratch_shapes=[pltpu.VMEM((SKETCH, SKETCH), F32)],
        compiler_params=pltpu.CompilerParams(vmem_limit_bytes=VMEM_LIMIT),
        name="basis",
    )(scalars, mine, theirs, own)


def project_kernel(bt_ref, w_ref, apart_ref, *out_refs):
    pieces, rows, depth = bt_ref.shape[1:]
    left = bt_ref[0].reshape(pieces * rows, depth)
    sums = jnp.sum(left.astype(F32), axis=1, keepdims=True)
    product = jnp.dot(left, w_ref[:depth, :], preferred_element_type=F32) + sums * apart_ref[...]
    product = product.astype(BF16)
    for k, out_ref in enumerate(out_refs):
        out_ref[...] = product[k * rows : (k + 1) * rows]


def project_call(basis, which, weighted, apart):
    _, pieces, rows, depth = basis.shape
    held, cols = weighted.shape
    block = 2048
    return pl.pallas_call(
        project_kernel,
        grid=(cols // block,),
        in_specs=[
            pl.BlockSpec((1, pieces, rows, depth), lambda i: (which, 0, 0, 0)),
            pl.BlockSpec((held, block), lambda i: (0, i)),
            pl.BlockSpec((1, block), lambda i: (0, i)),
        ],
        out_specs=[pl.BlockSpec((rows, block), lambda i: (0, i))] * pieces,
        out_shape=[jax.ShapeDtypeStruct((rows, cols), BF16)] * pieces,
        compiler_params=pltpu.CompilerParams(vmem_limit_bytes=VMEM_LIMIT),
        name="project",
    )(basis, weighted, apart)


def swap(value):
    return lax.ppermute(value, "core", [(0, 1), (1, 0)])


def shift_x(value, by):
    return lax.ppermute(value, "x", [(i, (i + by) % 4) for i in range(4)])


def body(counts, doc_freq, sketch_seed):
    rows, cols = counts.shape
    terms_axes = ("y", "z")
    parts = lax.axis_size(terms_axes)
    docs = lax.axis_size("x")
    my_x, my_core = lax.axis_index("x"), lax.axis_index("core")
    first_term = lax.axis_index(terms_axes) * cols
    scalars = jnp.stack([sketch_seed[0], first_term.astype(I32)])
    places = jnp.stack([my_x, my_core]).astype(I32)

    sketch_part, weighted, log_sums = sketch_call(scalars, counts, doc_freq)

    chunk = 2 * rows // parts
    pieces = lax.all_to_all(sketch_part.reshape(parts, chunk, LANES), terms_axes, 0, 0)
    share = jnp.sum(pieces, axis=0)
    block = jnp.concatenate([share, log_sums], axis=0)
    block = lax.all_to_all(jnp.broadcast_to(block[None], (docs,) + block.shape), "x", 0, 0)
    held = block[:, :chunk].reshape(docs * chunk, LANES)
    core_sums = jnp.sum(block[:, chunk:], axis=0)
    other_sums = swap(core_sums)

    centre = jnp.mean(held, axis=0, keepdims=True)
    sent = jnp.concatenate(
        [(held - centre).astype(BF16), *three_parts(centre), jnp.zeros((TAIL - 3, LANES), BF16)], axis=0
    )
    gathered = lax.all_to_all(jnp.broadcast_to(sent[None], (parts,) + sent.shape), terms_axes, 0, 0)
    mine, own = gram_call(places, gathered, rows)
    basis, flipped = basis_call(places, mine, swap(mine), own)

    log_mean = (core_sums + other_sums) * (1.0 / (rows * docs * lax.axis_size("core")))
    idf = idf_of(doc_freq)
    column_mean = idf * (1.0 + log_mean.reshape(cols))
    apart = idf * (log_sums * (1.0 / rows) - log_mean).reshape(cols)
    apart = apart.reshape(1, cols)

    theirs = project_call(flipped, 1, weighted, apart)
    theirs = [swap(piece) for piece in theirs]
    ours = project_call(flipped, 0, weighted, apart)
    sums = [(a.astype(F32) + b.astype(F32)).astype(BF16) for a, b in zip(ours, theirs)]
    total = sums[0].astype(F32)
    for by in (2, 1, 3):
        total = total + shift_x(sums[by], by).astype(F32)
    return (basis, total.astype(BF16), column_mean)


def solution(mesh):
    split = Mesh(np.array(mesh.devices).reshape(4, 2, 4, 8), ("x", "core", "y", "z"))
    docs, terms = ("x", "core"), ("y", "z")
    return jax.shard_map(
        body,
        mesh=split,
        in_specs=(P(docs, terms), P(terms), P()),
        out_specs=(P(docs, None), P(docs, terms), P(terms)),
        check_vma=False,
    )
```

time: 397 us -> 145 us (0.37)
  waiting for transfers between devices: 247 us -> 43.9 us
  other arithmetic: 67.3 us -> 2.4 us
  Pallas kernels: 0 us -> 42.7 us
  matrix products: 34 us -> 0 us
  starting transfers between devices: 0.3 us -> 19.4 us
  between operations: 15.8 us -> 1.39 us
  blocking collectives: 23.6 us -> 32.4 us
  local copies, waits for them, and re-layouts: 6 us -> 1.99 us
    psum x2 -> x0, waiting for transfers between devices: 209 us -> none  [the longest x1 144 us: body(): sketch = lax.psum(partial_value, 'term')]
    another operation x9 -> x2, other arithmetic: 53.7 us -> 0.15 us  [the longest x1 0.08 us: body(): scalars = jnp.stack([sketch_seed[0], first_term.astype(I32)])]
    pallas_call x0 -> x5, Pallas kernels: none -> 42.7 us  [the longest x1 15.9 us: sketch_call(): pl.pallas_call(sketch_kernel, grid=(cols // block,), in_specs=[pl.BlockSp...]
    reduce_scatter x1 -> x0, waiting for transfers between devices: 37.9 us -> none  [body(): lax.psum_scatter(jnp.dot(basis_left, weighted, preferred_element_type=jnp...]
    all_to_all x0 -> x2, blocking collectives: none -> 32.4 us  [the longest x1 23.5 us: body(): lax.all_to_all(sketch_part.reshape(parts, chunk, LANES), terms_axes, 0, 0)]
    dot_general x3 -> x0, matrix products: 30.4 us -> none  [the longest x1 15.5 us: body(): jnp.dot(weighted, test_matrix, preferred_element_type=jnp.float32)]
    ppermute x0 -> x9, waiting for transfers between devices: none -> 24 us  [the longest x3 22 us: shift_x(): return lax.ppermute(value, 'x', [(i, (i + by) % 4) for i in range(4)])]
    psum x1 -> x0, blocking collectives: 23.6 us -> none  [body(): column_total = lax.psum(jnp.sum(tfidf, axis=0), 'doc')]
  transfers between devices with their start and end apart: 3 -> 10, of which waited for: 3 -> 6; matrix products, arithmetic and copies ran while one was open for 0% -> 1% of each run, Pallas kernels for 0% -> 3%
where the time goes in v1:
time: 145 us; the launch traced here: 144 us
  waiting for transfers between devices  43.9 us (30%)
  Pallas kernels  42.7 us (29%)
  blocking collectives  32.4 us (22%)
  starting transfers between devices  19.4 us (13%)
  other arithmetic  2.4 us (2%)
  local copies, waits for them, and re-layouts  1.99 us (1%)
    all_to_all x1, blocking collectives, body(): lax.all_to_all(sketch_part.reshape(parts, chunk, LANES), terms_axes, 0, 0)  23.5 us
    ppermute x3, waiting for transfers between devices, shift_x(): return lax.ppermute(value, 'x', [(i, (i + by) % 4) for i in range(4)])  22 us
    all_to_all x1, waiting for transfers between devices, body(): lax.all_to_all(jnp.broadcast_to(sent[None], (parts,) + sent.shape), terms...  19.9 us
    pallas_call x1, Pallas kernels, sketch_call(): pl.pallas_call(sketch_kernel, grid=(cols // block,), in_specs=[pl.BlockSp...  15.9 us
    pallas_call x1, Pallas kernels, basis_call(): pl.pallas_call(basis_kernel, in_specs=[pl.BlockSpec(memory_space=pltpu.SM...  15.3 us
    pallas_call x2, Pallas kernels, project_call(): pl.pallas_call(project_kernel, grid=(cols // block,), in_specs=[pl.BlockS...  8.94 us
    all_to_all x1, blocking collectives, body(): lax.all_to_all(jnp.broadcast_to(block[None], (docs,) + block.shape), 'x',...  8.9 us
    ppermute x6, starting transfers between devices, swap(): return lax.ppermute(value, 'core', [(0, 1), (1, 0)])  8.31 us
  transfers between devices with their start and end apart: 10, of which 6 were waited for; matrix products, arithmetic and copies ran while one was open for 1% of the time, Pallas kernels for 3%

profile of v1, /device:TPU:1, one launch (start us, length us, event | category | flops | bytes accessed | tf_op | source)
XLA Modules:
  0.0 144.2 jit_solution(14214558234893832568)
XLA Ops:
  1.4 0.8 copy-done
  2.1 15.9 %sketch.1 = (f32[768,128]{1,0:T(8,128)S(1)}, bf16[400,8192]{1,0:T(8,128)(2,1)}, f32[64,128]{1,0:T(8,128)S(1)}) custom-call(s32[2]{0:T(128)S(1)} %pad_add_fusion.1.scal_ref, s32[384,8192]{1,0:T(8,128)} %counts_ref.1, s32[1,8192]{1,0:T(1,128)S(1)} %bitcast.30), custom_call_target="tpu_custom_call" | custom-call | tf_op jit(solution)/shard_map/sketch/pallas_call | solution.py:99
  18.1 23.5 %all_to_all.15 = f32[32,24,128]{2,1,0:T(8,128)S(1)} all-to-all(f32[32,24,128]{2,1,0:T(8,128)S(1)} %bitcast.27), channel_id=1, replica_groups=mesh['x'=4,'core'=2,'y'=4,'z'=8] {'y','z'}, dimensions={0} | all-to-all | bytes 786432 | tf_op jit(solution)/shard_map/all_to_all | solution.py:287
  41.6 8.9 %all_to_all.16 = f32[4,88,128]{2,1,0:T(8,128)S(1)} all-to-all(f32[4,88,128]{2,1,0:T(8,128)S(1)} %broadcast_in_dim.6), channel_id=1, replica_groups=mesh['x'=4,'core'=2,'y'=4,'z'=8] {'x'}, dimensions={0} | all-to-all | bytes 360448 | tf_op jit(solution)/shard_map/all_to_all | solution.py:290
  50.7 1.1 broadcast_in_dim.8
  51.8 7.5 %all-to-all-start.2 = ((bf16[32,112,128]{2,1,0:T(8,128)(2,1)}), bf16[32,112,128]{2,1,0:T(8,128)(2,1)S(1)}, u32[]{:S(2)}, u32[]{:S(2)}) async-start(bf16[32,112,128]{2,1,0:T(8,128)(2,1)} %broadcast_in_dim.8), calls=%async_computation.2 | async-start | bytes 1835008 | tf_op jit(solution)/shard_map/all_to_all | solution.py:299
  59.3 19.9 %all-to-all-done.2.g_ref = bf16[32,112,128]{2,1,0:T(8,128)(2,1)S(1)} async-done(((bf16[32,112,128]{2,1,0:T(8,128)(2,1)}), bf16[32,112,128]{2,1,0:T(8,128)(2,1)S(1)}, u32[]{:S(2)}, u32[]{:S(2)}) %all-to-all-start.2) | async-done | bytes 917536 | tf_op jit(solution)/shard_map/all_to_all | solution.py:299
  79.2 2.5 %gram.1 = (f32[264,256]{1,0:T(8,128)S(1)}, f32[384,256]{1,0:T(8,128)S(1)}) custom-call(s32[2]{0:T(128)S(1)} %pad_add_fusion.scal_ref, bf16[32,112,128]{2,1,0:T(8,128)(2,1)S(1)} %all-to-all-done.2.g_ref), custom_call_target="tpu_custom_call" | custom-call | tf_op jit(solution)/shard_map/gram/pallas_call | solution.py:150
  81.7 6.8 %collective-permute-start = (f32[264,256]{1,0:T(8,128)S(1)}, f32[264,256]{1,0:T(8,128)S(1)}, u32[]{:S(2)}, u32[]{:S(2)}) collective-permute-start(f32[264,256]{1,0:T(8,128)S(1)} %get-tuple-element.20.mine_ref), channel_id=1, source_target_pairs={{0,32},{32,0},{1,33},{33,1},{2,34},{34,2},{3,35},{35,3},{4,36},{36... | collective-permute-start | bytes 811016 | tf_op jit(solution)/shard_map/ppermute | solution.py:267
  88.6 0.3 collective-permute-start.1
  88.9 1.2 collective-permute-done.1
  90.0 0.6 bitcast_multiply_fusion
  90.7 15.3 %basis.1 = (f32[384,256]{1,0:T(8,128)}, bf16[2,4,32,384]{3,2,1,0:T(8,128)(2,1)S(1)}) custom-call(s32[2]{0:T(128)S(1)} %pad_add_fusion.scal_ref, f32[264,256]{1,0:T(8,128)S(1)} %get-tuple-element.20.mine_ref, f32[264,256]{1,0:T(8,128)S(1)} %collective-permute-done.theirs_ref, f32[384,256]{1,0:T(8,128)S(1)} %get-tuple-element.21.own_ref), custom_call_target="tpu_custom_call" | custom-call | tf_op jit(solution)/shard_map/basis/pallas_call | solution.py:223
  106.0 4.5 %project.3 = (bf16[32,8192]{1,0:T(8,128)(2,1)S(1)}, bf16[32,8192]{1,0:T(8,128)(2,1)S(1)}, bf16[32,8192]{1,0:T(8,128)(2,1)S(1)}, bf16[32,8192]{1,0:T(8,128)(2,1)S(1)}) custom-call(bf16[2,4,32,384]{3,2,1,0:T(8,128)(2,1)S(1)} %get-tuple-element.23.bt_ref, bf16[400,8192]{1,0:T(8,128)(2,1)} %get-tuple-element.24.w_ref, f32[1,8192]{1,0:T(1,128)S(1)} %bitcast.28), custom_call_target="tpu_custom_call" | custom-call | tf_op jit(solution)/shard_map/project/pallas_call | solution.py:251
  110.7 4.5 %project.2 = (bf16[32,8192]{1,0:T(8,128)(2,1)S(1)}, bf16[32,8192]{1,0:T(8,128)(2,1)S(1)}, bf16[32,8192]{1,0:T(8,128)(2,1)S(1)}, bf16[32,8192]{1,0:T(8,128)(2,1)S(1)}) custom-call(bf16[2,4,32,384]{3,2,1,0:T(8,128)(2,1)S(1)} %get-tuple-element.23.bt_ref, bf16[400,8192]{1,0:T(8,128)(2,1)} %get-tuple-element.24.w_ref, f32[1,8192]{1,0:T(1,128)S(1)} %bitcast.29), custom_call_target="tpu_custom_call" | custom-call | tf_op jit(solution)/shard_map/project/pallas_call | solution.py:251
  115.2 0.5 collective-permute-start.2
  115.8 0.4 collective-permute-start.7
  116.3 1.0 collective-permute-start.4
  117.4 0.6 collective-permute-done.5
  118.1 0.4 collective-permute-start.6
  118.8 2.2 %collective-permute-start.8 = (bf16[32,8192]{1,0:T(8,128)(2,1)S(1)}, bf16[32,8192]{1,0:T(8,128)(2,1)S(1)}, u32[]{:S(2)}, u32[]{:S(2)}) collective-permute-start(bf16[32,8192]{1,0:T(8,128)(2,1)S(1)} %add_convert_fusion.1), channel_id=1, source_target_pairs={{0,192},{64,0},{128,64},{192,128},{1,193},{65,1},{129,65},{193,129... | collective-permute-start | bytes 1572872 | tf_op jit(solution)/shard_map/ppermute | solution.py:271
  121.1 10.3 %collective-permute-done.4 = bf16[32,8192]{1,0:T(8,128)(2,1)S(1)} collective-permute-done((bf16[32,8192]{1,0:T(8,128)(2,1)S(1)}, bf16[32,8192]{1,0:T(8,128)(2,1)S(1)}, u32[]{:S(2)}, u32[]{:S(2)}) %collective-permute-start.4) | collective-permute-done | bytes 524320 | tf_op jit(solution)/shard_map/ppermute | solution.py:271
  131.3 11.7 %collective-permute-done.6 = bf16[32,8192]{1,0:T(8,128)(2,1)S(1)} collective-permute-done((bf16[32,8192]{1,0:T(8,128)(2,1)S(1)}, bf16[32,8192]{1,0:T(8,128)(2,1)S(1)}, u32[]{:S(2)}, u32[]{:S(2)}) %collective-permute-start.6) | collective-permute-done | bytes 524320 | tf_op jit(solution)/shard_map/ppermute | solution.py:271
  143.0 1.1 add_convert_fusion
  (25 shorter events, 1.4 us)
Async XLA Ops:
  1.4 0.8 copy-start
  2.1 87.9 %copy-start.1 = (s32[8192]{0:T(1024)S(1)}, s32[8192]{0:T(1024)}, u32[]{:S(2)}) copy-start(s32[8192]{0:T(1024)} %param.4) | copy-start | bytes 98308
  51.8 27.4 %all-to-all-start.2 = ((bf16[32,112,128]{2,1,0:T(8,128)(2,1)}), bf16[32,112,128]{2,1,0:T(8,128)(2,1)S(1)}, u32[]{:S(2)}, u32[]{:S(2)}) async-start(bf16[32,112,128]{2,1,0:T(8,128)(2,1)} %broadcast_in_dim.8), calls=%async_computation.2 | async-start | bytes 1835008 | tf_op jit(solution)/shard_map/all_to_all | solution.py:299
  81.7 9.0 %collective-permute-start = (f32[264,256]{1,0:T(8,128)S(1)}, f32[264,256]{1,0:T(8,128)S(1)}, u32[]{:S(2)}, u32[]{:S(2)}) collective-permute-start(f32[264,256]{1,0:T(8,128)S(1)} %get-tuple-element.20.mine_ref), channel_id=1, source_target_pairs={{0,32},{32,0},{1,33},{33,1},{2,34},{34,2},{3,35},{35,3},{4,36},{36... | collective-permute-start | bytes 811016 | tf_op jit(solution)/shard_map/ppermute | solution.py:267
  88.6 1.5 %collective-permute-start.1 = (f32[64,128]{1,0:T(8,128)S(1)}, f32[64,128]{1,0:T(8,128)S(1)}, u32[]{:S(2)}, u32[]{:S(2)}) collective-permute-start(f32[64,128]{1,0:T(8,128)S(1)} %slice_reduce_fusion), channel_id=1, source_target_pairs={{0,32},{32,0},{1,33},{33,1},{2,34},{34,2},{3,35},{35,3},{4,36},{36... | collective-permute-start | bytes 98312 | tf_op jit(solution)/shard_map/ppermute | solution.py:267
  110.5 5.7 %collective-permute-start.3 = (bf16[32,8192]{1,0:T(8,128)(2,1)S(1)}, bf16[32,8192]{1,0:T(8,128)(2,1)S(1)}, u32[]{:S(2)}, u32[]{:S(2)}) collective-permute-start(bf16[32,8192]{1,0:T(8,128)(2,1)S(1)} %get-tuple-element.28), channel_id=1, source_target_pairs={{0,32},{32,0},{1,33},{33,1},{2,34},{34,2},{3,35},{35,3},{4,36},{36... | collective-permute-start | bytes 1572872 | tf_op jit(solution)/shard_map/ppermute | solution.py:267
  115.2 5.9 %collective-permute-start.2 = (bf16[32,8192]{1,0:T(8,128)(2,1)S(1)}, bf16[32,8192]{1,0:T(8,128)(2,1)S(1)}, u32[]{:S(2)}, u32[]{:S(2)}) collective-permute-start(bf16[32,8192]{1,0:T(8,128)(2,1)S(1)} %get-tuple-element.26), channel_id=1, source_target_pairs={{0,32},{32,0},{1,33},{33,1},{2,34},{34,2},{3,35},{35,3},{4,36},{36... | collective-permute-start | bytes 1572872 | tf_op jit(solution)/shard_map/ppermute | solution.py:267
  115.7 2.3 %collective-permute-start.5 = (bf16[32,8192]{1,0:T(8,128)(2,1)S(1)}, bf16[32,8192]{1,0:T(8,128)(2,1)S(1)}, u32[]{:S(2)}, u32[]{:S(2)}) collective-permute-start(bf16[32,8192]{1,0:T(8,128)(2,1)S(1)} %get-tuple-element.30), channel_id=1, source_target_pairs={{0,32},{32,0},{1,33},{33,1},{2,34},{34,2},{3,35},{35,3},{4,36},{36... | collective-permute-start | bytes 1572872 | tf_op jit(solution)/shard_map/ppermute | solution.py:267
  115.8 2.9 %collective-permute-start.7 = (bf16[32,8192]{1,0:T(8,128)(2,1)S(1)}, bf16[32,8192]{1,0:T(8,128)(2,1)S(1)}, u32[]{:S(2)}, u32[]{:S(2)}) collective-permute-start(bf16[32,8192]{1,0:T(8,128)(2,1)S(1)} %get-tuple-element.32), channel_id=1, source_target_pairs={{0,32},{32,0},{1,33},{33,1},{2,34},{34,2},{3,35},{35,3},{4,36},{36... | collective-permute-start | bytes 1572872 | tf_op jit(solution)/shard_map/ppermute | solution.py:267
  116.3 15.0 %collective-permute-start.4 = (bf16[32,8192]{1,0:T(8,128)(2,1)S(1)}, bf16[32,8192]{1,0:T(8,128)(2,1)S(1)}, u32[]{:S(2)}, u32[]{:S(2)}) collective-permute-start(bf16[32,8192]{1,0:T(8,128)(2,1)S(1)} %add_convert_fusion.3), channel_id=1, source_target_pairs={{0,128},{64,192},{128,0},{192,64},{1,129},{65,193},{129,1},{193,65... | collective-permute-start | bytes 1572872 | tf_op jit(solution)/shard_map/ppermute | solution.py:271
  118.1 24.9 %collective-permute-start.6 = (bf16[32,8192]{1,0:T(8,128)(2,1)S(1)}, bf16[32,8192]{1,0:T(8,128)(2,1)S(1)}, u32[]{:S(2)}, u32[]{:S(2)}) collective-permute-start(bf16[32,8192]{1,0:T(8,128)(2,1)S(1)} %add_convert_fusion.2), channel_id=1, source_target_pairs={{0,64},{64,128},{128,192},{192,0},{1,65},{65,129},{129,193},{193,1... | collective-permute-start | bytes 1572872 | tf_op jit(solution)/shard_map/ppermute | solution.py:271
  118.8 24.2 %collective-permute-start.8 = (bf16[32,8192]{1,0:T(8,128)(2,1)S(1)}, bf16[32,8192]{1,0:T(8,128)(2,1)S(1)}, u32[]{:S(2)}, u32[]{:S(2)}) collective-permute-start(bf16[32,8192]{1,0:T(8,128)(2,1)S(1)} %add_convert_fusion.1), channel_id=1, source_target_pairs={{0,192},{64,0},{128,64},{192,128},{1,193},{65,1},{129,65},{193,129... | collective-permute-start | bytes 1572872 | tf_op jit(solution)/shard_map/ppermute | solution.py:271

commit v2 on v0

v2 whole, which is shorter than its diff:
```python
import functools
import math

import jax
import jax.numpy as jnp
import numpy as np
from jax import lax
from jax.experimental import pallas as pl
from jax.experimental.pallas import tpu as pltpu
from jax.sharding import Mesh
from jax.sharding import PartitionSpec as P

TERMS = 262144
SKETCH = 256
CORPUS = 2000000000
BYTE_SUM_STD = 147.8
FACTOR = 1.0 / (BYTE_SUM_STD * TERMS**0.5)
HIGHEST = lax.Precision.HIGHEST
F32, BF16, I32 = jnp.float32, jnp.bfloat16, jnp.int32
VMEM_LIMIT = 16 * 1024 * 1024
LANES = 128
PIVOTS = 32
TAIL = 16
MEAN_ROWS = 8
TRIANGLE = 192
MEANS = 16


def log_count(counts):
    return jnp.log(jnp.maximum(counts.astype(F32), math.exp(-1.0)))


def idf_of(doc_freq):
    return 1.0 + jnp.log(jnp.float32(CORPUS) / doc_freq.astype(F32))


def three_parts(value):
    high = value.astype(BF16)
    rest = value - high.astype(F32)
    middle = rest.astype(BF16)
    low = (rest - middle.astype(F32)).astype(BF16)
    return high, middle, low


def parts_tile(value, rows):
    high, middle, low = (part.astype(F32) for part in three_parts(value))
    where = lax.broadcasted_iota(I32, (rows, value.shape[1]), 0)
    tile = jnp.where(where == 0, high, jnp.where(where == 1, middle, jnp.where(where == 2, low, 0.0)))
    return tile.astype(BF16)


def sketch_kernel(
    seed_ref, counts_hbm, df_hbm, s_ref, w_hbm, lsum_ref, centre_ref, idf, counts, df, om, wb, in_sems, out_sems, df_sem
):
    rows, cols = counts_hbm.shape
    strip = rows // in_sems.shape[0]
    chunk = cols // out_sems.shape[0]

    def load(i):
        at = pl.ds(i * strip, strip)
        return pltpu.make_async_copy(counts_hbm.at[at], counts.at[at], in_sems.at[i])

    def store(i):
        at = pl.ds(pl.multiple_of(i * chunk, chunk), chunk)
        return pltpu.make_async_copy(wb.at[:, at], w_hbm.at[:, at], out_sems.at[i])

    load_df = pltpu.make_async_copy(df_hbm, df, df_sem)
    load_df.start()
    for i in range(rows // strip):
        load(i).start()

    first = lax.axis_index(("y", "z")) * (cols * SKETCH)
    key = seed_ref[0] * 668265263
    low_key, high_key = key & 255, key & -256
    lane = lax.broadcasted_iota(I32, (1, LANES), 1)
    col_parts = [((lane + half * LANES) ^ low_key) * 1640531527 for half in range(SKETCH // LANES)]
    group = 256
    local = lax.broadcasted_iota(I32, (group, LANES), 0) * SKETCH + first

    def hash_rows(g, carry):
        row_part = ((local + g * (group * SKETCH)) ^ high_key) * 1640531527
        for half, col_part in enumerate(col_parts):
            h = row_part + col_part
            h = h ^ lax.shift_right_logical(h, jnp.int32(15))
            h = h * 739982445
            h = h ^ lax.shift_right_logical(h, jnp.int32(13))
            pair = (h & 0x00FF00FF) + (lax.shift_right_logical(h, jnp.int32(8)) & 0x00FF00FF)
            byte_sum = lax.shift_right_logical(pair * 65537, jnp.int32(16))
            value = (byte_sum - 510).astype(F32).astype(BF16)
            om[pl.ds(pl.multiple_of(g * group, group), group), half * LANES : (half + 1) * LANES] = value
        return carry

    lax.fori_loop(0, cols // group, hash_rows, 0)

    load_df.wait()
    idf[...] = idf_of(df[...])
    for i in range(rows // strip):
        load(i).wait()

    strip_rows = 32

    def weigh(tile):
        at = pl.ds(pl.multiple_of(tile * LANES, LANES), LANES)
        part = log_count(counts[:strip_rows, at])
        centre = jnp.sum(part, axis=0, keepdims=True) * (1.0 / strip_rows)
        scale = idf[pl.ds(tile, 1), :]
        wb[:strip_rows, at] = ((part - centre) * scale).astype(BF16)
        wb[rows:, at] = parts_tile(scale * (1.0 + centre), TAIL)
        centre_ref[pl.ds(tile, 1), :] = centre
        for r in range(strip_rows, rows, strip_rows):
            values = log_count(counts[r : r + strip_rows, at])
            part = part + values
            wb[r : r + strip_rows, at] = ((values - centre) * scale).astype(BF16)
        lsum_ref[pl.ds(tile, 1), :] = jnp.sum(part, axis=0, keepdims=True)

    def weigh_chunk(i, carry):
        per_chunk = chunk // LANES

        def one(k, c):
            weigh(i * per_chunk + k)
            return c

        lax.fori_loop(0, per_chunk, one, 0, unroll=2)
        store(i).start()
        return carry

    lax.fori_loop(0, cols // chunk, weigh_chunk, 0)

    product = jnp.dot(wb[...], om[...], preferred_element_type=F32) * FACTOR
    centre = jnp.sum(product[rows:, :], axis=0, keepdims=True)
    shares = s_ref.shape[0] // 2
    share = rows // shares
    for half in range(SKETCH // LANES):
        at = slice(half * LANES, (half + 1) * LANES)
        tail = parts_tile(centre[:, at], MEAN_ROWS).astype(F32)
        for t in range(shares):
            value = jnp.concatenate([product[share * t : share * (t + 1), at], tail], axis=0)
            s_ref[shares * half + t] = value.astype(BF16)
    for i in range(cols // chunk):
        store(i).wait()


def sketch_call(seed, counts, doc_freq, parts):
    rows, cols = counts.shape
    in_vmem = pl.BlockSpec(memory_space=pltpu.VMEM)
    in_hbm = pl.BlockSpec(memory_space=pltpu.HBM)
    return pl.pallas_call(
        sketch_kernel,
        in_specs=[pl.BlockSpec(memory_space=pltpu.SMEM), in_hbm, in_hbm],
        out_specs=[in_vmem, in_hbm, in_vmem, in_vmem, in_vmem],
        out_shape=[
            pltpu.VMEM((parts, 2 * rows // parts + MEAN_ROWS, LANES), BF16),
            pltpu.HBM((rows + TAIL, cols), BF16),
        ]
        + [jax.ShapeDtypeStruct((cols // LANES, LANES), F32)] * 3,
        scratch_shapes=[
            pltpu.VMEM((rows, cols), I32),
            pltpu.VMEM((cols // LANES, LANES), I32),
            pltpu.VMEM((cols, SKETCH), BF16),
            pltpu.VMEM((rows + TAIL, cols), BF16),
            pltpu.SemaphoreType.DMA((8,)),
            pltpu.SemaphoreType.DMA((8,)),
            pltpu.SemaphoreType.DMA,
        ],
        compiler_params=pltpu.CompilerParams(vmem_limit_bytes=40 * 1024 * 1024),
        name="sketch",
    )(
        seed,
        pltpu.with_memory_space_constraint(counts, pltpu.HBM),
        pltpu.with_memory_space_constraint(doc_freq.reshape(cols // LANES, LANES), pltpu.HBM),
    )


def share_kernel(pieces_ref, out_ref):
    total = pieces_ref[0].astype(F32)
    for t in range(1, pieces_ref.shape[0]):
        total = total + pieces_ref[t].astype(F32)
    held = total.shape[0] - MEAN_ROWS
    centre = total[held : held + 1] + total[held + 1 : held + 2] + total[held + 2 : held + 3]
    value = jnp.concatenate([total[:held], parts_tile(centre, MEAN_ROWS).astype(F32)], axis=0).astype(BF16)
    for t in range(out_ref.shape[0]):
        out_ref[t] = value


def share_call(pieces):
    return pl.pallas_call(
        share_kernel,
        in_specs=[pl.BlockSpec(memory_space=pltpu.VMEM)],
        out_specs=pl.BlockSpec(memory_space=pltpu.VMEM),
        out_shape=pltpu.VMEM(pieces.shape, BF16),
        compiler_params=pltpu.CompilerParams(vmem_limit_bytes=VMEM_LIMIT),
        name="share",
    )(pieces)


def gram_kernel(scal_ref, g_ref, lsum_ref, pay_ref, own_ref):
    my_x, my_core = scal_ref[0], scal_ref[1]
    parts, held, _ = g_ref.shape
    half_parts = parts // 2
    held -= MEAN_ROWS
    rows = held * half_parts
    for t in range(half_parts):
        for half in range(2):
            block = g_ref[t + half_parts * half].astype(F32)
            mean = block[held : held + 1] + block[held + 1 : held + 2] + block[held + 2 : held + 3]
            own_ref[held * t : held * (t + 1), half * LANES : (half + 1) * LANES] = block[:held] + mean
    full = own_ref[...]
    mean = jnp.sum(full, axis=0, keepdims=True) * (1.0 / rows)
    centred = full - mean
    own_ref[...] = centred
    gram = lax.dot_general(centred, centred, (((0,), (0,)), ((), ())), precision=HIGHEST, preferred_element_type=F32)
    row = lax.broadcasted_iota(I32, (MEANS, LANES), 0) - (4 * my_x + 2 * my_core)
    means = jnp.where(row == 0, mean[:, :LANES], jnp.where(row == 1, mean[:, LANES:], 0.0))
    sums = lsum_ref.shape[0] // 2
    for half in range(2):
        at = my_core ^ half
        pay_ref[at, :LANES] = gram[LANES * half : LANES * (half + 1), LANES * half : LANES * (half + 1)]
        pay_ref[at, LANES:TRIANGLE] = gram[64 * half : 64 * (half + 1), LANES:]
        pay_ref[at, TRIANGLE : TRIANGLE + MEANS] = means
        pay_ref[at, TRIANGLE + MEANS :] = lsum_ref[sums * half : sums * (half + 1)]


def gram_call(scalars, gathered, log_sums, rows):
    return pl.pallas_call(
        gram_kernel,
        in_specs=[pl.BlockSpec(memory_space=pltpu.SMEM)] + [pl.BlockSpec(memory_space=pltpu.VMEM)] * 2,
        out_specs=[pl.BlockSpec(memory_space=pltpu.VMEM)] * 2,
        out_shape=[
            jax.ShapeDtypeStruct((2, TRIANGLE + MEANS + log_sums.shape[0] // 2, LANES), F32),
            jax.ShapeDtypeStruct((rows, SKETCH), F32),
        ],
        compiler_params=pltpu.CompilerParams(vmem_limit_bytes=VMEM_LIMIT),
        name="gram",
    )(scalars, gathered, log_sums)


def stacked(value):
    high, middle, low = three_parts(value)
    left = jnp.concatenate([high, high, middle, high, low, middle], axis=0)
    right = jnp.concatenate([high, middle, high, low, high, middle], axis=0)
    return left, right


def over_rows(left, right):
    return lax.dot_general(left, right, (((0,), (0,)), ((), ())), preferred_element_type=F32)


def eliminate(panel, start):
    count, tile = panel.shape[0], 8
    tiles = count // tile
    lane = lax.broadcasted_iota(I32, (tile, LANES), 1)
    sub = lax.broadcasted_iota(I32, (tile, LANES), 0)
    rows = [panel[tile * t : tile * (t + 1)] for t in range(tiles)]
    spread = [
        [
            jnp.broadcast_to(rows[t][:, start + k : start + k + 1], (tile, LANES)) if t >= k // tile else None
            for t in range(tiles)
        ]
        for k in range(count)
    ]
    halves = []
    for half in range(SKETCH // LANES):
        pieces = [row[:, half * LANES : (half + 1) * LANES] for row in rows]
        if start // LANES == half:
            local = lane - (start - half * LANES)
            for t in range(tiles):
                unit = jnp.where(local == sub + tile * t, 1.0, 0.0)
                pieces[t] = jnp.where((local >= 0) & (local < count), unit, pieces[t])
        halves.append(pieces)
    pivots = [jnp.zeros((tile, LANES), F32) for _ in range(tiles)]
    for j in range(count):
        at, row = j // tile, j % tile
        pivot = jnp.broadcast_to(spread[j][at][row : row + 1], (tile, LANES))
        pivots[at] = jnp.where(sub == row, pivot, pivots[at])
        if j + 1 == count:
            break
        inverse = 1.0 / pivot
        scale = [None if t < at else spread[j][t] * inverse for t in range(tiles)]
        scale[at] = jnp.where(sub > row, scale[at], 0.0)
        for k in range(j + 1, count):
            factor = spread[j][k // tile][k % tile : k % tile + 1]
            for t in range(k // tile, tiles):
                spread[k][t] = spread[k][t] - scale[t] * factor
        for pieces in halves:
            factor = pieces[at][row : row + 1]
            for t in range(at, tiles):
                pieces[t] = pieces[t] - scale[t] * factor
    roots = [lax.rsqrt(pivot) for pivot in pivots]
    return jnp.concatenate(
        [jnp.concatenate([pieces[t] * roots[t] for t in range(tiles)], axis=0) for pieces in halves], axis=1
    )


def basis_kernel(scal_ref, mine_ref, theirs_ref, own_ref, w_hbm, q_ref, bt_ref, w_ref, work, sem):
    fetch = pltpu.make_async_copy(w_hbm, w_ref, sem)
    fetch.start()
    my_x, my_core = scal_ref[0], scal_ref[1]
    size = SKETCH

    @pl.when(my_core >= 0)
    def _():
        mine, theirs = mine_ref[...], theirs_ref[...]
        first = jnp.where(my_core == 0, mine, theirs)
        second = jnp.where(my_core == 0, theirs, mine)
        means = mine[TRIANGLE : TRIANGLE + MEANS]
        mean_rows = [means[2 * d : 2 * d + 2] for d in range(8)]
        centre = sum(mean_rows) * 0.125
        apart = [jnp.concatenate([m[0:1] - centre[0:1], m[1:2] - centre[1:2]], axis=1) for m in mean_rows]
        apart = jnp.concatenate(apart, axis=0)
        docs = own_ref.shape[0]
        shift = over_rows(*stacked(jnp.concatenate([apart, jnp.zeros_like(apart)], axis=0))) * jnp.float32(docs)
        work[:LANES, :LANES] = first[:LANES] + shift[:LANES, :LANES]
        work[:64, LANES:] = first[LANES:TRIANGLE] + shift[:64, LANES:]
        work[64:LANES, LANES:] = second[LANES:TRIANGLE] + shift[64:LANES, LANES:]
        work[LANES:, LANES:] = second[:LANES] + shift[LANES:, LANES:]
        work[LANES:, :LANES] = jnp.zeros((LANES, LANES), F32)
        mean_at = lax.broadcasted_iota(I32, (8, SKETCH), 0) == 2 * my_x + my_core
        own_shift = jnp.sum(jnp.where(mean_at, apart, 0.0), axis=0, keepdims=True)

        for start in range(0, size, PIVOTS):
            rest = start + PIVOTS
            factor_rows = eliminate(work[start:rest, :], start)
            work[start:rest, :] = factor_rows
            if rest < size:
                left, right = stacked(factor_rows)
                from_col = rest // LANES * LANES
                update = over_rows(left[:, from_col:], right)
                old = work[rest:, :]
                column = lax.broadcasted_iota(I32, old.shape, 1)
                old = jnp.where((column >= start) & (column < rest), 0.0, old)
                work[rest:, :] = old - update[rest - from_col :, :]

        row = lax.broadcasted_iota(I32, (size, size), 0)
        column = lax.broadcasted_iota(I32, (size, size), 1)
        inverse = jnp.where(column <= row, work[...], 0.0)
        own = own_ref[...] + own_shift
        contract = (((1,), (1,)), ((), ()))
        q_ref[...] = lax.dot_general(own, inverse, contract, precision=HIGHEST, preferred_element_type=F32)
        flipped = lax.dot_general(inverse, own, contract, precision=HIGHEST, preferred_element_type=F32).astype(BF16)
        rows = size // 8
        for x in range(4):
            place = (x - my_x) & 3
            place = jnp.where(place == 2, 0, jnp.where(place == 3, 2, jnp.where(place == 1, 1, 3)))
            for core in range(2):
                piece = flipped[rows * (2 * x + core) : rows * (2 * x + core + 1)]
                bt_ref[place, (my_core + core) & 1] = piece

    fetch.wait()


def basis_call(scalars, mine, theirs, own, weighted):
    rows = own.shape[0]
    in_vmem = pl.BlockSpec(memory_space=pltpu.VMEM)
    in_hbm = pl.BlockSpec(memory_space=pltpu.HBM)
    return pl.pallas_call(
        basis_kernel,
        in_specs=[pl.BlockSpec(memory_space=pltpu.SMEM)] + [in_vmem] * 3 + [in_hbm],
        out_specs=[in_vmem] * 3,
        out_shape=[
            jax.ShapeDtypeStruct((rows, SKETCH), F32),
            jax.ShapeDtypeStruct((4, 2, SKETCH // 8, rows), BF16),
            pltpu.VMEM(weighted.shape, BF16),
        ],
        scratch_shapes=[pltpu.VMEM((SKETCH, SKETCH), F32), pltpu.SemaphoreType.DMA],
        compiler_params=pltpu.CompilerParams(vmem_limit_bytes=VMEM_LIMIT),
        name="basis",
    )(scalars, mine, theirs, own, pltpu.with_memory_space_constraint(weighted, pltpu.HBM))


def project_kernel(scal_ref, bt_ref, w_ref, centre_ref, idf_ref, mine_ref, theirs_ref, *out_refs, first):
    _, cores, rows, depth = bt_ref.shape
    ours_refs, sibling_refs, mean_ref = out_refs[:-1:2], out_refs[1:-1:2], out_refs[-1]
    pieces = len(ours_refs)
    width = ours_refs[0].shape[1]
    left = bt_ref[first : first + pieces].reshape(pieces * cores * rows, depth)
    sums = jnp.sum(left.astype(F32), axis=1, keepdims=True)
    tail = TRIANGLE + MEANS
    on_first = scal_ref[1] == 0
    low = jnp.where(on_first, mine_ref[tail:], theirs_ref[tail:])
    high = jnp.where(on_first, theirs_ref[tail:], mine_ref[tail:])
    log_mean = jnp.concatenate([low, high], axis=0) * (1.0 / (8 * depth))
    idf = idf_ref[...]
    mean_ref[...] = idf * (1.0 + log_mean)
    apart = idf * (centre_ref[...] - log_mean)
    block = 512
    for at in range(0, width, block):
        product = jnp.dot(left, w_ref[:depth, at : at + block], preferred_element_type=F32)
        row = at // LANES
        shift = jnp.concatenate([apart[row + k : row + k + 1] for k in range(block // LANES)], axis=1)
        product = (product + sums * shift).astype(BF16)
        for k in range(pieces):
            base = k * cores * rows
            ours_refs[k][:, at : at + block] = product[base : base + rows]
            sibling_refs[k][:, at : at + block] = product[base + rows : base + 2 * rows]


def project_call(places, basis, weighted, centres, idf, mine, theirs, first, pieces):
    _, _, rows, _ = basis.shape
    cols = weighted.shape[1]
    in_vmem = pl.BlockSpec(memory_space=pltpu.VMEM)
    return pl.pallas_call(
        functools.partial(project_kernel, first=first),
        in_specs=[pl.BlockSpec(memory_space=pltpu.SMEM)] + [in_vmem] * 6,
        out_specs=[in_vmem] * (2 * pieces + 1),
        out_shape=[jax.ShapeDtypeStruct((rows, cols), BF16)] * (2 * pieces)
        + [jax.ShapeDtypeStruct(centres.shape, F32)],
        compiler_params=pltpu.CompilerParams(vmem_limit_bytes=24 * 1024 * 1024),
        name="project",
    )(places, basis, weighted, centres, idf, mine, theirs)


def swap(value):
    return lax.ppermute(value, "core", [(0, 1), (1, 0)])


def shift_x(value, by):
    return lax.ppermute(value, "x", [(i, (i + by) % 4) for i in range(4)])


def half_sum(a, b):
    return (a.astype(F32) + b.astype(F32)).astype(BF16)


def body(counts, doc_freq, sketch_seed):
    rows, cols = counts.shape
    terms_axes = ("y", "z")
    parts = lax.axis_size(terms_axes)
    my_x, my_core = lax.axis_index("x"), lax.axis_index("core")
    places = jnp.stack([my_x, my_core]).astype(I32)

    sketch_part, weighted, log_sums, centres, idf = sketch_call(sketch_seed, counts, doc_freq, parts)

    pieces = lax.all_to_all(sketch_part, terms_axes, 0, 0)
    gathered = lax.all_to_all(share_call(pieces), terms_axes, 0, 0)
    payload, own = gram_call(places, gathered, log_sums, rows)

    mine = payload[0] + swap(payload[1])
    mine = (mine + shift_x(mine, 2)) + (shift_x(mine, 1) + shift_x(mine, 3))
    theirs = swap(mine)
    basis, flipped, weighted = basis_call(places, mine, theirs, own, weighted)

    operands = (places, flipped, weighted, centres, idf, mine, theirs)
    ours2, other2, means = project_call(*operands, 0, 1)
    opposite = half_sum(ours2, swap(other2))
    flipped, opposite = lax.optimization_barrier((flipped, opposite))
    operands = (places, flipped) + operands[2:]
    ours1, other1, ours3, other3, _ = project_call(*operands, 1, 2)
    flipped, other1, other3 = lax.optimization_barrier((flipped, other1, other3))
    operands = (places, flipped) + operands[2:]
    ours0, other0, _ = project_call(*operands, 3, 1)
    half = cols // 2
    relay_up = shift_x(opposite[:, :half], 1)
    relay_down = shift_x(opposite[:, half:], -1)
    up = ours1.astype(F32) + swap(other1).astype(F32)
    up = jnp.concatenate([up[:, :half] + relay_up.astype(F32), up[:, half:]], axis=1).astype(BF16)
    down = ours3.astype(F32) + swap(other3).astype(F32)
    down = jnp.concatenate([down[:, :half], down[:, half:] + relay_down.astype(F32)], axis=1).astype(BF16)
    total = ours0.astype(F32) + swap(other0).astype(F32)
    total = total + shift_x(up, 1).astype(F32) + shift_x(down, -1).astype(F32)
    return (basis, total.astype(BF16), means.reshape(cols))


def solution(mesh):
    split = Mesh(np.array(mesh.devices).reshape(4, 2, 4, 8), ("x", "core", "y", "z"))
    docs, terms = ("x", "core"), ("y", "z")
    return jax.shard_map(
        body,
        mesh=split,
        in_specs=(P(docs, terms), P(terms), P()),
        out_specs=(P(docs, None), P(docs, terms), P(terms)),
        check_vma=False,
    )
```

time: 397 us -> 111 us (0.28)
  waiting for transfers between devices: 247 us -> 32.3 us
  other arithmetic: 67.3 us -> 1.68 us
  matrix products: 34 us -> 0 us
  Pallas kernels: 0 us -> 29.3 us
  starting transfers between devices: 0.3 us -> 23.8 us
  between operations: 15.8 us -> 1.43 us
  local copies, waits for them, and re-layouts: 6 us -> 0.1 us
    psum x2 -> x0, waiting for transfers between devices: 209 us -> none  [the longest x1 144 us: body(): sketch = lax.psum(partial_value, 'term')]
    another operation x9 -> x3, other arithmetic: 53.7 us -> 0.17 us  [the longest x6 34 us: body(): lower_factor = jnp.linalg.cholesky(gram_matrix)]
    reduce_scatter x1 -> x0, waiting for transfers between devices: 37.9 us -> none  [body(): lax.psum_scatter(jnp.dot(basis_left, weighted, preferred_element_type=jnp...]
    dot_general x3 -> x0, matrix products: 30.4 us -> none  [the longest x1 15.5 us: body(): jnp.dot(weighted, test_matrix, preferred_element_type=jnp.float32)]
    pallas_call x0 -> x7, Pallas kernels: none -> 29.3 us  [the longest x1 11.4 us: sketch_call(): pl.pallas_call(sketch_kernel, in_specs=[pl.BlockSpec(memory_space=pltpu.S...]
    psum x1 -> x0, blocking collectives: 23.6 us -> none  [body(): column_total = lax.psum(jnp.sum(tfidf, axis=0), 'doc')]
    ppermute x0 -> x13, waiting for transfers between devices: none -> 22.7 us  [the longest x7 19.2 us: shift_x(): return lax.ppermute(value, 'x', [(i, (i + by) % 4) for i in range(4)])]
    all_to_all x0 -> x1, blocking collectives: none -> 21.5 us  [body(): pieces = lax.all_to_all(sketch_part, terms_axes, 0, 0)]
  transfers between devices with their start and end apart: 3 -> 14, of which waited for: 3 -> 9; matrix products, arithmetic and copies ran while one was open for 0% -> 0% of each run, Pallas kernels for 0% -> 2%
where the time goes in v2:
time: 111 us; the launch traced here: 110 us
  waiting for transfers between devices  32.3 us (29%)
  Pallas kernels  29.3 us (26%)
  starting transfers between devices  23.8 us (21%)
  blocking collectives  21.5 us (19%)
  other arithmetic  1.68 us (2%)
  between operations  1.43 us (1%)
    all_to_all x1, blocking collectives, body(): pieces = lax.all_to_all(sketch_part, terms_axes, 0, 0)  21.5 us
    ppermute x7, waiting for transfers between devices, shift_x(): return lax.ppermute(value, 'x', [(i, (i + by) % 4) for i in range(4)])  19.2 us
    pallas_call x1, Pallas kernels, sketch_call(): pl.pallas_call(sketch_kernel, in_specs=[pl.BlockSpec(memory_space=pltpu.S...  11.4 us
    ppermute x7, starting transfers between devices, shift_x(): return lax.ppermute(value, 'x', [(i, (i + by) % 4) for i in range(4)])  9.85 us
    all_to_all x1, waiting for transfers between devices, body(): gathered = lax.all_to_all(share_call(pieces), terms_axes, 0, 0)  9.58 us
    pallas_call x1, Pallas kernels, basis_call(): pl.pallas_call(basis_kernel, in_specs=[pl.BlockSpec(memory_space=pltpu.SM...  8.96 us
    ppermute x6, starting transfers between devices, swap(): return lax.ppermute(value, 'core', [(0, 1), (1, 0)])  7.68 us
    pallas_call x3, Pallas kernels, project_call(): pl.pallas_call(functools.partial(project_kernel, first=first), in_specs=[...  6.98 us
  transfers between devices with their start and end apart: 14, of which 9 were waited for; matrix products, arithmetic and copies ran while one was open for 0% of the time, Pallas kernels for 2%

profile of v2, /device:TPU:1, one launch (start us, length us, event | category | flops | bytes accessed | tf_op | source)
XLA Modules:
  0.0 110.1 jit_solution(13413565834734941954)
XLA Ops:
  1.3 11.4 %sketch.1 = (bf16[32,32,128]{2,1,0:T(8,128)(2,1)S(1)}, bf16[400,8192]{1,0:T(8,128)(2,1)}, f32[64,128]{1,0:T(8,128)S(1)}, f32[64,128]{1,0:T(8,128)S(1)}, f32[64,128]{1,0:T(8,128)S(1)}) custom-call(s32[1]{0:T(128)S(6)} %copy.6.seed_ref, s32[384,8192]{1,0:T(8,128)} %counts_hbm.1, s32[64,128]{1,0:T(8,128)} %bitcast.8), custom_call_target="tpu_custom_call" | custom-call | tf_op jit(solution)/shard_map/sketch/pallas_call | solution.py:147
  12.6 21.5 %all_to_all.10.pieces_ref = bf16[32,32,128]{2,1,0:T(8,128)(2,1)S(1)} all-to-all(bf16[32,32,128]{2,1,0:T(8,128)(2,1)S(1)} %get-tuple-element.27), channel_id=1, replica_groups=mesh['x'=4,'core'=2,'y'=4,'z'=8] {'y','z'}, dimensions={0} | all-to-all | bytes 524288 | tf_op jit(solution)/shard_map/all_to_all | solution.py:433
  34.2 0.8 share.1
  34.9 6.3 %all-to-all-start.1 = ((bf16[32,32,128]{2,1,0:T(8,128)(2,1)}), bf16[32,32,128]{2,1,0:T(8,128)(2,1)S(1)}, u32[]{:S(2)}, u32[]{:S(2)}) async-start(bf16[32,32,128]{2,1,0:T(8,128)(2,1)} %share.1), calls=%async_computation.1 | async-start | bytes 524288 | tf_op jit(solution)/shard_map/all_to_all | solution.py:434
  41.3 9.6 %all-to-all-done.1.g_ref = bf16[32,32,128]{2,1,0:T(8,128)(2,1)S(1)} async-done(((bf16[32,32,128]{2,1,0:T(8,128)(2,1)}), bf16[32,32,128]{2,1,0:T(8,128)(2,1)S(1)}, u32[]{:S(2)}, u32[]{:S(2)}) %all-to-all-start.1) | async-done | bytes 262176 | tf_op jit(solution)/shard_map/all_to_all | solution.py:434
  50.9 1.3 %gram.1 = (f32[2,240,128]{2,1,0:T(8,128)S(1)}, f32[384,256]{1,0:T(8,128)S(1)}) custom-call(s32[2]{0:T(128)S(1)} %pad_add_fusion.scal_ref, bf16[32,32,128]{2,1,0:T(8,128)(2,1)S(1)} %all-to-all-done.1.g_ref, f32[64,128]{1,0:T(8,128)S(1)} %get-tuple-element.28.lsum_ref), custom_call_target="tpu_custom_call" | custom-call | tf_op jit(solution)/shard_map/gram/pallas_call | solution.py:224
  52.2 3.7 %collective-permute-start = (f32[240,128]{1,0:T(8,128)S(1)}, f32[240,128]{1,0:T(8,128)S(1)}, u32[]{:S(2)}, u32[]{:S(2)}) collective-permute-start(f32[240,128]{1,0:T(8,128)S(1)} %slice_bitcast_fusion), channel_id=1, source_target_pairs={{0,32},{32,0},{1,33},{33,1},{2,34},{34,2},{3,35},{35,3},{4,36},{36... | collective-permute-start | bytes 368648 | tf_op jit(solution)/shard_map/ppermute | solution.py:413
  55.9 1.0 collective-permute-done
  56.9 2.6 %collective-permute-start.3 = (f32[240,128]{1,0:T(8,128)S(1)}, f32[240,128]{1,0:T(8,128)S(1)}, u32[]{:S(2)}, u32[]{:S(2)}) collective-permute-start(f32[240,128]{1,0:T(8,128)S(1)} %bitcast_add_fusion), channel_id=1, source_target_pairs={{0,192},{64,0},{128,64},{192,128},{1,193},{65,1},{129,65},{193,129... | collective-permute-start | bytes 368648 | tf_op jit(solution)/shard_map/ppermute | solution.py:417
  59.4 1.7 %collective-permute-start.1 = (f32[240,128]{1,0:T(8,128)S(1)}, f32[240,128]{1,0:T(8,128)S(1)}, u32[]{:S(2)}, u32[]{:S(2)}) collective-permute-start(f32[240,128]{1,0:T(8,128)S(1)} %bitcast_add_fusion), channel_id=1, source_target_pairs={{0,128},{64,192},{128,0},{192,64},{1,129},{65,193},{129,1},{193,65... | collective-permute-start | bytes 368648 | tf_op jit(solution)/shard_map/ppermute | solution.py:417
  61.8 4.5 %collective-permute-done.2 = f32[240,128]{1,0:T(8,128)S(1)} collective-permute-done((f32[240,128]{1,0:T(8,128)S(1)}, f32[240,128]{1,0:T(8,128)S(1)}, u32[]{:S(2)}, u32[]{:S(2)}) %collective-permute-start.2) | collective-permute-done | bytes 122912 | tf_op jit(solution)/shard_map/ppermute | solution.py:417
  66.6 2.5 %collective-permute-start.4 = (f32[240,128]{1,0:T(8,128)S(1)}, f32[240,128]{1,0:T(8,128)S(1)}, u32[]{:S(2)}, u32[]{:S(2)}) collective-permute-start(f32[240,128]{1,0:T(8,128)S(1)} %add_add_fusion.mine_ref), channel_id=1, source_target_pairs={{0,32},{32,0},{1,33},{33,1},{2,34},{34,2},{3,35},{35,3},{4,36},{36... | collective-permute-start | bytes 368648 | tf_op jit(solution)/shard_map/ppermute | solution.py:413
  69.1 1.0 collective-permute-done.4.theirs_ref
  70.1 9.0 %basis.1 = (f32[384,256]{1,0:T(8,128)}, bf16[4,2,32,384]{3,2,1,0:T(8,128)(2,1)S(1)}, bf16[400,8192]{1,0:T(8,128)(2,1)S(1)}) custom-call(s32[2]{0:T(128)S(1)} %pad_add_fusion.scal_ref, f32[240,128]{1,0:T(8,128)S(1)} %add_add_fusion.mine_ref, f32[240,128]{1,0:T(8,128)S(1)} %collective-permute-done.4.theirs_ref, f32[384,256]{1,0:T(8,128)S(1)} %get-tuple-element.30.own_ref, ...), custom_call_target="tpu_custom_call" | custom-call | tf_op jit(solution)/shard_map/basis/pallas_call | solution.py:355
  79.1 2.3 %project.3 = (bf16[32,8192]{1,0:T(8,128)(2,1)S(1)}, bf16[32,8192]{1,0:T(8,128)(2,1)S(1)}, f32[64,128]{1,0:T(8,128)}) custom-call(s32[2]{0:T(128)S(1)} %pad_add_fusion.scal_ref, bf16[4,2,32,384]{3,2,1,0:T(8,128)(2,1)S(1)} %get-tuple-element.42.bt_ref, bf16[400,8192]{1,0:T(8,128)(2,1)S(1)} %get-tuple-element.34.w_ref, ...), custom_call_target="tpu_custom_call" | custom-call | tf_op jit(solution)/shard_map/project/pallas_call | solution.py:401
  81.7 1.5 %collective-permute-done.5 = bf16[32,8192]{1,0:T(8,128)(2,1)S(1)} collective-permute-done((bf16[32,8192]{1,0:T(8,128)(2,1)S(1)}, bf16[32,8192]{1,0:T(8,128)(2,1)S(1)}, u32[]{:S(2)}, u32[]{:S(2)}) %collective-permute-start.5) | collective-permute-done | bytes 524320 | tf_op jit(solution)/shard_map/ppermute | solution.py:413
  83.4 2.4 %project.4 = (bf16[32,8192]{1,0:T(8,128)(2,1)S(1)}, bf16[32,8192]{1,0:T(8,128)(2,1)S(1)}, bf16[32,8192]{1,0:T(8,128)(2,1)S(1)}, bf16[32,8192]{1,0:T(8,128)(2,1)S(1)}, f32[64,128]{1,0:T(8,128)}) custom-call(s32[2]{0:T(128)S(1)} %pad_add_fusion.scal_ref, bf16[4,2,32,384]{3,2,1,0:T(8,128)(2,1)S(1)} %get-tuple-element.42.bt_ref, ...), custom_call_target="tpu_custom_call" | custom-call | tf_op jit(solution)/shard_map/project/pallas_call | solution.py:401
  86.3 2.7 %collective-permute-start.11 = (bf16[32,4096]{1,0:T(8,128)(2,1)S(1)}, bf16[32,4096]{1,0:T(8,128)(2,1)S(1)}, u32[]{:S(2)}, u32[]{:S(2)}) collective-permute-start(bf16[32,4096]{1,0:T(8,128)(2,1)S(1)} %get-tuple-element.52), channel_id=1, source_target_pairs={{0,192},{64,0},{128,64},{192,128},{1,193},{65,1},{129,65},{193,129... | collective-permute-start | bytes 786440 | tf_op jit(solution)/shard_map/ppermute | solution.py:417
  88.9 2.3 %project.5 = (bf16[32,8192]{1,0:T(8,128)(2,1)S(1)}, bf16[32,8192]{1,0:T(8,128)(2,1)S(1)}, f32[64,128]{1,0:T(8,128)}) custom-call(s32[2]{0:T(128)S(1)} %pad_add_fusion.scal_ref, bf16[4,2,32,384]{3,2,1,0:T(8,128)(2,1)S(1)} %get-tuple-element.42.bt_ref, bf16[400,8192]{1,0:T(8,128)(2,1)S(1)} %get-tuple-element.34.w_ref, ...), custom_call_target="tpu_custom_call" | custom-call | tf_op jit(solution)/shard_map/project/pallas_call | solution.py:401
  91.2 0.7 collective-permute-start.6
  92.1 3.1 %collective-permute-done.8 = bf16[32,4096]{1,0:T(8,128)(2,1)S(1)} collective-permute-done((bf16[32,4096]{1,0:T(8,128)(2,1)S(1)}, bf16[32,4096]{1,0:T(8,128)(2,1)S(1)}, u32[]{:S(2)}, u32[]{:S(2)}) %collective-permute-start.8) | collective-permute-done | bytes 262176 | tf_op jit(solution)/shard_map/ppermute | solution.py:417
  95.7 2.7 %collective-permute-start.12 = (bf16[32,8192]{1,0:T(8,128)(2,1)S(1)}, bf16[32,8192]{1,0:T(8,128)(2,1)S(1)}, u32[]{:S(2)}, u32[]{:S(2)}) collective-permute-start(bf16[32,8192]{1,0:T(8,128)(2,1)S(1)} %pad_maximum_fusion.1), channel_id=1, source_target_pairs={{0,192},{64,0},{128,64},{192,128},{1,193},{65,1},{129,65},{193,129... | collective-permute-start | bytes 1572872 | tf_op jit(solution)/shard_map/ppermute | solution.py:417
  98.4 10.7 %collective-permute-done.9 = bf16[32,8192]{1,0:T(8,128)(2,1)S(1)} collective-permute-done((bf16[32,8192]{1,0:T(8,128)(2,1)S(1)}, bf16[32,8192]{1,0:T(8,128)(2,1)S(1)}, u32[]{:S(2)}, u32[]{:S(2)}) %collective-permute-start.9) | collective-permute-done | bytes 524320 | tf_op jit(solution)/shard_map/ppermute | solution.py:417
  109.1 1.1 add_convert_fusion
  (27 shorter events, 2.6 us)
Async XLA Ops:
  34.9 16.0 %all-to-all-start.1 = ((bf16[32,32,128]{2,1,0:T(8,128)(2,1)}), bf16[32,32,128]{2,1,0:T(8,128)(2,1)S(1)}, u32[]{:S(2)}, u32[]{:S(2)}) async-start(bf16[32,32,128]{2,1,0:T(8,128)(2,1)} %share.1), calls=%async_computation.1 | async-start | bytes 524288 | tf_op jit(solution)/shard_map/all_to_all | solution.py:434
  52.2 4.7 %collective-permute-start = (f32[240,128]{1,0:T(8,128)S(1)}, f32[240,128]{1,0:T(8,128)S(1)}, u32[]{:S(2)}, u32[]{:S(2)}) collective-permute-start(f32[240,128]{1,0:T(8,128)S(1)} %slice_bitcast_fusion), channel_id=1, source_target_pairs={{0,32},{32,0},{1,33},{33,1},{2,34},{34,2},{3,35},{35,3},{4,36},{36... | collective-permute-start | bytes 368648 | tf_op jit(solution)/shard_map/ppermute | solution.py:413
  56.9 4.9 %collective-permute-start.3 = (f32[240,128]{1,0:T(8,128)S(1)}, f32[240,128]{1,0:T(8,128)S(1)}, u32[]{:S(2)}, u32[]{:S(2)}) collective-permute-start(f32[240,128]{1,0:T(8,128)S(1)} %bitcast_add_fusion), channel_id=1, source_target_pairs={{0,192},{64,0},{128,64},{192,128},{1,193},{65,1},{129,65},{193,129... | collective-permute-start | bytes 368648 | tf_op jit(solution)/shard_map/ppermute | solution.py:417
  59.4 6.8 %collective-permute-start.2 = (f32[240,128]{1,0:T(8,128)S(1)}, f32[240,128]{1,0:T(8,128)S(1)}, u32[]{:S(2)}, u32[]{:S(2)}) collective-permute-start(f32[240,128]{1,0:T(8,128)S(1)} %bitcast_add_fusion), channel_id=1, source_target_pairs={{0,64},{64,128},{128,192},{192,0},{1,65},{65,129},{129,193},{193,1... | collective-permute-start | bytes 368648 | tf_op jit(solution)/shard_map/ppermute | solution.py:417
  59.4 7.1 %collective-permute-start.1 = (f32[240,128]{1,0:T(8,128)S(1)}, f32[240,128]{1,0:T(8,128)S(1)}, u32[]{:S(2)}, u32[]{:S(2)}) collective-permute-start(f32[240,128]{1,0:T(8,128)S(1)} %bitcast_add_fusion), channel_id=1, source_target_pairs={{0,128},{64,192},{128,0},{192,64},{1,129},{65,193},{129,1},{193,65... | collective-permute-start | bytes 368648 | tf_op jit(solution)/shard_map/ppermute | solution.py:417
  66.6 3.5 %collective-permute-start.4 = (f32[240,128]{1,0:T(8,128)S(1)}, f32[240,128]{1,0:T(8,128)S(1)}, u32[]{:S(2)}, u32[]{:S(2)}) collective-permute-start(f32[240,128]{1,0:T(8,128)S(1)} %add_add_fusion.mine_ref), channel_id=1, source_target_pairs={{0,32},{32,0},{1,33},{33,1},{2,34},{34,2},{3,35},{35,3},{4,36},{36... | collective-permute-start | bytes 368648 | tf_op jit(solution)/shard_map/ppermute | solution.py:413
  81.4 1.9 %collective-permute-start.5 = (bf16[32,8192]{1,0:T(8,128)(2,1)S(1)}, bf16[32,8192]{1,0:T(8,128)(2,1)S(1)}, u32[]{:S(2)}, u32[]{:S(2)}) collective-permute-start(bf16[32,8192]{1,0:T(8,128)(2,1)S(1)} %get-tuple-element.38), channel_id=1, source_target_pairs={{0,32},{32,0},{1,33},{33,1},{2,34},{34,2},{3,35},{35,3},{4,36},{36... | collective-permute-start | bytes 1572872 | tf_op jit(solution)/shard_map/ppermute | solution.py:413
  85.8 6.2 %collective-permute-start.7 = (bf16[32,8192]{1,0:T(8,128)(2,1)S(1)}, bf16[32,8192]{1,0:T(8,128)(2,1)S(1)}, u32[]{:S(2)}, u32[]{:S(2)}) collective-permute-start(bf16[32,8192]{1,0:T(8,128)(2,1)S(1)} %get-tuple-element.46), channel_id=1, source_target_pairs={{0,32},{32,0},{1,33},{33,1},{2,34},{34,2},{3,35},{35,3},{4,36},{36... | collective-permute-start | bytes 1572872 | tf_op jit(solution)/shard_map/ppermute | solution.py:413
  86.2 9.0 %collective-permute-start.8 = (bf16[32,4096]{1,0:T(8,128)(2,1)S(1)}, bf16[32,4096]{1,0:T(8,128)(2,1)S(1)}, u32[]{:S(2)}, u32[]{:S(2)}) collective-permute-start(bf16[32,4096]{1,0:T(8,128)(2,1)S(1)} %get-tuple-element.51), channel_id=1, source_target_pairs={{0,64},{64,128},{128,192},{192,0},{1,65},{65,129},{129,193},{193,1... | collective-permute-start | bytes 786440 | tf_op jit(solution)/shard_map/ppermute | solution.py:417
  86.3 9.3 %collective-permute-start.11 = (bf16[32,4096]{1,0:T(8,128)(2,1)S(1)}, bf16[32,4096]{1,0:T(8,128)(2,1)S(1)}, u32[]{:S(2)}, u32[]{:S(2)}) collective-permute-start(bf16[32,4096]{1,0:T(8,128)(2,1)S(1)} %get-tuple-element.52), channel_id=1, source_target_pairs={{0,192},{64,0},{128,64},{192,128},{1,193},{65,1},{129,65},{193,129... | collective-permute-start | bytes 786440 | tf_op jit(solution)/shard_map/ppermute | solution.py:417
  91.2 7.2 %collective-permute-start.6 = (bf16[32,8192]{1,0:T(8,128)(2,1)S(1)}, bf16[32,8192]{1,0:T(8,128)(2,1)S(1)}, u32[]{:S(2)}, u32[]{:S(2)}) collective-permute-start(bf16[32,8192]{1,0:T(8,128)(2,1)S(1)} %get-tuple-element.44), channel_id=1, source_target_pairs={{0,32},{32,0},{1,33},{33,1},{2,34},{34,2},{3,35},{35,3},{4,36},{36... | collective-permute-start | bytes 1572872 | tf_op jit(solution)/shard_map/ppermute | solution.py:413
  92.0 3.5 %collective-permute-start.10 = (bf16[32,8192]{1,0:T(8,128)(2,1)S(1)}, bf16[32,8192]{1,0:T(8,128)(2,1)S(1)}, u32[]{:S(2)}, u32[]{:S(2)}) collective-permute-start(bf16[32,8192]{1,0:T(8,128)(2,1)S(1)} %get-tuple-element.49), channel_id=1, source_target_pairs={{0,32},{32,0},{1,33},{33,1},{2,34},{34,2},{3,35},{35,3},{4,36},{36... | collective-permute-start | bytes 1572872 | tf_op jit(solution)/shard_map/ppermute | solution.py:413
  95.3 13.8 %collective-permute-start.9 = (bf16[32,8192]{1,0:T(8,128)(2,1)S(1)}, bf16[32,8192]{1,0:T(8,128)(2,1)S(1)}, u32[]{:S(2)}, u32[]{:S(2)}) collective-permute-start(bf16[32,8192]{1,0:T(8,128)(2,1)S(1)} %pad_maximum_fusion), channel_id=1, source_target_pairs={{0,64},{64,128},{128,192},{192,0},{1,65},{65,129},{129,193},{193,1... | collective-permute-start | bytes 1572872 | tf_op jit(solution)/shard_map/ppermute | solution.py:417
  95.7 13.4 %collective-permute-start.12 = (bf16[32,8192]{1,0:T(8,128)(2,1)S(1)}, bf16[32,8192]{1,0:T(8,128)(2,1)S(1)}, u32[]{:S(2)}, u32[]{:S(2)}) collective-permute-start(bf16[32,8192]{1,0:T(8,128)(2,1)S(1)} %pad_maximum_fusion.1), channel_id=1, source_target_pairs={{0,192},{64,0},{128,64},{192,128},{1,193},{65,1},{129,65},{193,129... | collective-permute-start | bytes 1572872 | tf_op jit(solution)/shard_map/ppermute | solution.py:417

commit v3 on v2

--- a/solution.py
+++ b/solution.py
@@ -193,8 +193,8 @@
     )(pieces)
 
 
-def gram_kernel(scal_ref, g_ref, lsum_ref, pay_ref, own_ref):
-    my_x, my_core = scal_ref[0], scal_ref[1]
+def gram_kernel(g_ref, lsum_ref, pay_ref, own_ref):
+    my_x, my_core = lax.axis_index("x"), lax.axis_index("core")
     parts, held, _ = g_ref.shape
     half_parts = parts // 2
     held -= MEAN_ROWS
@@ -220,10 +220,10 @@
         pay_ref[at, TRIANGLE + MEANS :] = lsum_ref[sums * half : sums * (half + 1)]
 
 
-def gram_call(scalars, gathered, log_sums, rows):
+def gram_call(gathered, log_sums, rows):
     return pl.pallas_call(
         gram_kernel,
-        in_specs=[pl.BlockSpec(memory_space=pltpu.SMEM)] + [pl.BlockSpec(memory_space=pltpu.VMEM)] * 2,
+        in_specs=[pl.BlockSpec(memory_space=pltpu.VMEM)] * 2,
         out_specs=[pl.BlockSpec(memory_space=pltpu.VMEM)] * 2,
         out_shape=[
             jax.ShapeDtypeStruct((2, TRIANGLE + MEANS + log_sums.shape[0] // 2, LANES), F32),
@@ -231,7 +231,7 @@
         ],
         compiler_params=pltpu.CompilerParams(vmem_limit_bytes=VMEM_LIMIT),
         name="gram",
-    )(scalars, gathered, log_sums)
+    )(gathered, log_sums)
 
 
 def stacked(value):
@@ -243,6 +243,10 @@
 
 def over_rows(left, right):
     return lax.dot_general(left, right, (((0,), (0,)), ((), ())), preferred_element_type=F32)
+
+
+def by_rows(left, right):
+    return lax.dot_general(left, right, (((1,), (1,)), ((), ())), precision=HIGHEST, preferred_element_type=F32)
 
 
 def eliminate(panel, start):
@@ -291,10 +295,10 @@
     )
 
 
-def basis_kernel(scal_ref, mine_ref, theirs_ref, own_ref, w_hbm, q_ref, bt_ref, w_ref, work, sem):
+def basis_kernel(mine_ref, theirs_ref, own_ref, w_hbm, inverse_ref, shifted_ref, bt_ref, w_ref, work, sem):
     fetch = pltpu.make_async_copy(w_hbm, w_ref, sem)
     fetch.start()
-    my_x, my_core = scal_ref[0], scal_ref[1]
+    my_x, my_core = lax.axis_index("x"), lax.axis_index("core")
     size = SKETCH
 
     @pl.when(my_core >= 0)
@@ -334,9 +338,9 @@
         column = lax.broadcasted_iota(I32, (size, size), 1)
         inverse = jnp.where(column <= row, work[...], 0.0)
         own = own_ref[...] + own_shift
-        contract = (((1,), (1,)), ((), ()))
-        q_ref[...] = lax.dot_general(own, inverse, contract, precision=HIGHEST, preferred_element_type=F32)
-        flipped = lax.dot_general(inverse, own, contract, precision=HIGHEST, preferred_element_type=F32).astype(BF16)
+        inverse_ref[...] = inverse
+        shifted_ref[...] = own
+        flipped = by_rows(inverse, own).astype(BF16)
         rows = size // 8
         for x in range(4):
             place = (x - my_x) & 3
@@ -348,15 +352,16 @@
     fetch.wait()
 
 
-def basis_call(scalars, mine, theirs, own, weighted):
+def basis_call(mine, theirs, own, weighted):
     rows = own.shape[0]
     in_vmem = pl.BlockSpec(memory_space=pltpu.VMEM)
     in_hbm = pl.BlockSpec(memory_space=pltpu.HBM)
     return pl.pallas_call(
         basis_kernel,
-        in_specs=[pl.BlockSpec(memory_space=pltpu.SMEM)] + [in_vmem] * 3 + [in_hbm],
-        out_specs=[in_vmem] * 3,
+        in_specs=[in_vmem] * 3 + [in_hbm],
+        out_specs=[in_vmem] * 4,
         out_shape=[
+            jax.ShapeDtypeStruct((SKETCH, SKETCH), F32),
             jax.ShapeDtypeStruct((rows, SKETCH), F32),
             jax.ShapeDtypeStruct((4, 2, SKETCH // 8, rows), BF16),
             pltpu.VMEM(weighted.shape, BF16),
@@ -364,49 +369,60 @@
         scratch_shapes=[pltpu.VMEM((SKETCH, SKETCH), F32), pltpu.SemaphoreType.DMA],
         compiler_params=pltpu.CompilerParams(vmem_limit_bytes=VMEM_LIMIT),
         name="basis",
-    )(scalars, mine, theirs, own, pltpu.with_memory_space_constraint(weighted, pltpu.HBM))
-
-
-def project_kernel(scal_ref, bt_ref, w_ref, centre_ref, idf_ref, mine_ref, theirs_ref, *out_refs, first):
+    )(mine, theirs, own, pltpu.with_memory_space_constraint(weighted, pltpu.HBM))
+
+
+def log_means(mine_ref, theirs_ref, docs):
+    tail = TRIANGLE + MEANS
+    on_first = lax.axis_index("core") == 0
+    low = jnp.where(on_first, mine_ref[tail:], theirs_ref[tail:])
+    high = jnp.where(on_first, theirs_ref[tail:], mine_ref[tail:])
+    return jnp.concatenate([low, high], axis=0) * (1.0 / docs)
+
+
+def project_kernel(bt_ref, w_ref, centre_ref, idf_ref, mine_ref, theirs_ref, *out_refs, first, pieces, cut):
     _, cores, rows, depth = bt_ref.shape
-    ours_refs, sibling_refs, mean_ref = out_refs[:-1:2], out_refs[1:-1:2], out_refs[-1]
-    pieces = len(ours_refs)
-    width = ours_refs[0].shape[1]
+    width = w_ref.shape[1]
     left = bt_ref[first : first + pieces].reshape(pieces * cores * rows, depth)
     sums = jnp.sum(left.astype(F32), axis=1, keepdims=True)
-    tail = TRIANGLE + MEANS
-    on_first = scal_ref[1] == 0
-    low = jnp.where(on_first, mine_ref[tail:], theirs_ref[tail:])
-    high = jnp.where(on_first, theirs_ref[tail:], mine_ref[tail:])
-    log_mean = jnp.concatenate([low, high], axis=0) * (1.0 / (8 * depth))
-    idf = idf_ref[...]
-    mean_ref[...] = idf * (1.0 + log_mean)
-    apart = idf * (centre_ref[...] - log_mean)
+    apart = idf_ref[...] * (centre_ref[...] - log_means(mine_ref, theirs_ref, 8 * depth))
     block = 512
     for at in range(0, width, block):
         product = jnp.dot(left, w_ref[:depth, at : at + block], preferred_element_type=F32)
         row = at // LANES
         shift = jnp.concatenate([apart[row + k : row + k + 1] for k in range(block // LANES)], axis=1)
         product = (product + sums * shift).astype(BF16)
-        for k in range(pieces):
-            base = k * cores * rows
-            ours_refs[k][:, at : at + block] = product[base : base + rows]
-            sibling_refs[k][:, at : at + block] = product[base + rows : base + 2 * rows]
-
-
-def project_call(places, basis, weighted, centres, idf, mine, theirs, first, pieces):
-    _, _, rows, _ = basis.shape
-    cols = weighted.shape[1]
+        for k in range(pieces * cores):
+            value = product[k * rows : (k + 1) * rows]
+            if not cut:
+                out_refs[k][:, at : at + block] = value
+            elif k >= cores:
+                out_refs[cores + k][:, at : at + block] = value
+            else:
+                begin = at % (width // 2)
+                out_refs[2 * (2 * at // width) + k][:, begin : begin + block] = value
+
+
+def project_last_kernel(own_ref, inverse_ref, bt_ref, w_ref, centre_ref, idf_ref, mine_ref, theirs_ref, *out_refs):
+    q_ref, mean_ref = out_refs[2:]
+    q_ref[...] = by_rows(own_ref[...], inverse_ref[...])
+    docs = 8 * own_ref.shape[0]
+    mean_ref[...] = idf_ref[...] * (1.0 + log_means(mine_ref, theirs_ref, docs))
+    project_kernel(
+        bt_ref, w_ref, centre_ref, idf_ref, mine_ref, theirs_ref, *out_refs[:2], first=3, pieces=1, cut=False
+    )
+
+
+def project_call(kernel, outs, operands):
     in_vmem = pl.BlockSpec(memory_space=pltpu.VMEM)
     return pl.pallas_call(
-        functools.partial(project_kernel, first=first),
-        in_specs=[pl.BlockSpec(memory_space=pltpu.SMEM)] + [in_vmem] * 6,
-        out_specs=[in_vmem] * (2 * pieces + 1),
-        out_shape=[jax.ShapeDtypeStruct((rows, cols), BF16)] * (2 * pieces)
-        + [jax.ShapeDtypeStruct(centres.shape, F32)],
+        kernel,
+        in_specs=[in_vmem] * len(operands),
+        out_specs=[in_vmem] * len(outs),
+        out_shape=outs,
         compiler_params=pltpu.CompilerParams(vmem_limit_bytes=24 * 1024 * 1024),
         name="project",
-    )(places, basis, weighted, centres, idf, mine, theirs)
+    )(*operands)
 
 
 def swap(value):
@@ -425,38 +441,40 @@
     rows, cols = counts.shape
     terms_axes = ("y", "z")
     parts = lax.axis_size(terms_axes)
-    my_x, my_core = lax.axis_index("x"), lax.axis_index("core")
-    places = jnp.stack([my_x, my_core]).astype(I32)
 
     sketch_part, weighted, log_sums, centres, idf = sketch_call(sketch_seed, counts, doc_freq, parts)
 
     pieces = lax.all_to_all(sketch_part, terms_axes, 0, 0)
     gathered = lax.all_to_all(share_call(pieces), terms_axes, 0, 0)
-    payload, own = gram_call(places, gathered, log_sums, rows)
+    payload, own = gram_call(gathered, log_sums, rows)
 
     mine = payload[0] + swap(payload[1])
     mine = (mine + shift_x(mine, 2)) + (shift_x(mine, 1) + shift_x(mine, 3))
     theirs = swap(mine)
-    basis, flipped, weighted = basis_call(places, mine, theirs, own, weighted)
-
-    operands = (places, flipped, weighted, centres, idf, mine, theirs)
-    ours2, other2, means = project_call(*operands, 0, 1)
-    opposite = half_sum(ours2, swap(other2))
-    flipped, opposite = lax.optimization_barrier((flipped, opposite))
-    operands = (places, flipped) + operands[2:]
-    ours1, other1, ours3, other3, _ = project_call(*operands, 1, 2)
-    flipped, other1, other3 = lax.optimization_barrier((flipped, other1, other3))
-    operands = (places, flipped) + operands[2:]
-    ours0, other0, _ = project_call(*operands, 3, 1)
+    inverse, own, flipped, weighted = basis_call(mine, theirs, own, weighted)
+
     half = cols // 2
-    relay_up = shift_x(opposite[:, :half], 1)
-    relay_down = shift_x(opposite[:, half:], -1)
-    up = ours1.astype(F32) + swap(other1).astype(F32)
+    narrow, wide = (jax.ShapeDtypeStruct((SKETCH // 8, n), BF16) for n in (half, cols))
+    rest = (weighted, centres, idf, mine, theirs)
+    ours2a, other2a, ours2b, other2b, ours1, other1, ours3, other3 = project_call(
+        functools.partial(project_kernel, first=0, pieces=3, cut=True), [narrow] * 4 + [wide] * 4, (flipped,) + rest
+    )
+    relay_up = shift_x(half_sum(ours2a, swap(other2a)), 1)
+    relay_down = shift_x(half_sum(ours2b, swap(other2b)), -1)
+    theirs1, theirs3 = swap(other1), swap(other3)
+    up = ours1.astype(F32) + theirs1.astype(F32)
     up = jnp.concatenate([up[:, :half] + relay_up.astype(F32), up[:, half:]], axis=1).astype(BF16)
-    down = ours3.astype(F32) + swap(other3).astype(F32)
+    down = ours3.astype(F32) + theirs3.astype(F32)
     down = jnp.concatenate([down[:, :half], down[:, half:] + relay_down.astype(F32)], axis=1).astype(BF16)
+    from_below, from_above = shift_x(up, 1), shift_x(down, -1)
+    flipped, _, _ = lax.optimization_barrier((flipped, theirs1, theirs3))
+    ours0, other0, basis, means = project_call(
+        project_last_kernel,
+        [wide, wide, jax.ShapeDtypeStruct(own.shape, F32), jax.ShapeDtypeStruct(idf.shape, F32)],
+        (own, inverse, flipped) + rest,
+    )
     total = ours0.astype(F32) + swap(other0).astype(F32)
-    total = total + shift_x(up, 1).astype(F32) + shift_x(down, -1).astype(F32)
+    total = total + from_below.astype(F32) + from_above.astype(F32)
     return (basis, total.astype(BF16), means.reshape(cols))
 
 

time: 111 us -> 104 us (0.937)
  blocking collectives: 21.5 us -> 37.3 us
  waiting for transfers between devices: 32.3 us -> 20.3 us
  Pallas kernels: 29.3 us -> 23.1 us
  starting transfers between devices: 23.8 us -> 19 us
    all_to_all x0 -> x1, blocking collectives: none -> 15.8 us  [body(): gathered = lax.all_to_all(share_call(pieces), terms_axes, 0, 0)]
    all_to_all x1 -> x0, waiting for transfers between devices: 9.58 us -> none  [body(): gathered = lax.all_to_all(share_call(pieces), terms_axes, 0, 0)]
    all_to_all x1 -> x0, starting transfers between devices: 6.29 us -> none  [body(): gathered = lax.all_to_all(share_call(pieces), terms_axes, 0, 0)]
    pallas_call x5 -> x4, Pallas kernels: 17.2 us -> 11.7 us  [the longest x1 7.16 us: basis_call(): pl.pallas_call(basis_kernel, in_specs=[in_vmem] * 3 + [in_hbm], out_specs...]
    ppermute x7, waiting for transfers between devices: 19.2 us -> 17.6 us  [shift_x(): return lax.ppermute(value, 'x', [(i, (i + by) % 4) for i in range(4)])]
    ppermute x6 -> x7, starting transfers between devices: 7.68 us -> 9.09 us  [swap(): return lax.ppermute(value, 'core', [(0, 1), (1, 0)])]
    ppermute x6 -> x7, waiting for transfers between devices: 3.51 us -> 2.69 us  [swap(): return lax.ppermute(value, 'core', [(0, 1), (1, 0)])]
  transfers between devices with their start and end apart: 14 -> 14, of which waited for: 9 -> 9; matrix products, arithmetic and copies ran while one was open for 0% -> 1% of each run, Pallas kernels for 2% -> 2%
where the time goes in v3:
time: 104 us; the launch traced here: 103 us
  blocking collectives  37.3 us (36%)
  Pallas kernels  23.1 us (22%)
  waiting for transfers between devices  20.3 us (20%)
  starting transfers between devices  19 us (18%)
  other arithmetic  1.61 us (2%)
  between operations  1.43 us (1%)
    all_to_all x1, blocking collectives, body(): pieces = lax.all_to_all(sketch_part, terms_axes, 0, 0)  21.5 us
    ppermute x7, waiting for transfers between devices, shift_x(): return lax.ppermute(value, 'x', [(i, (i + by) % 4) for i in range(4)])  17.6 us
    all_to_all x1, blocking collectives, body(): gathered = lax.all_to_all(share_call(pieces), terms_axes, 0, 0)  15.8 us
    pallas_call x1, Pallas kernels, sketch_call(): pl.pallas_call(sketch_kernel, in_specs=[pl.BlockSpec(memory_space=pltpu.S...  11.4 us
    ppermute x7, starting transfers between devices, shift_x(): return lax.ppermute(value, 'x', [(i, (i + by) % 4) for i in range(4)])  9.93 us
    ppermute x7, starting transfers between devices, swap(): return lax.ppermute(value, 'core', [(0, 1), (1, 0)])  9.09 us
    pallas_call x1, Pallas kernels, basis_call(): pl.pallas_call(basis_kernel, in_specs=[in_vmem] * 3 + [in_hbm], out_specs...  7.16 us
    pallas_call x2, Pallas kernels, project_call(): pl.pallas_call(kernel, in_specs=[in_vmem] * len(operands), out_specs=[in_...  3.81 us
  transfers between devices with their start and end apart: 14, of which 9 were waited for; matrix products, arithmetic and copies ran while one was open for 1% of the time, Pallas kernels for 2%

profile of v3, /device:TPU:1, one launch (start us, length us, event | category | flops | bytes accessed | tf_op | source)
XLA Modules:
  0.0 102.8 jit_solution(2088789483890929426)
XLA Ops:
  1.3 11.4 %sketch.1 = (bf16[32,32,128]{2,1,0:T(8,128)(2,1)S(1)}, bf16[400,8192]{1,0:T(8,128)(2,1)}, f32[64,128]{1,0:T(8,128)S(1)}, f32[64,128]{1,0:T(8,128)S(1)}, f32[64,128]{1,0:T(8,128)S(1)}) custom-call(s32[1]{0:T(128)S(6)} %copy.6.seed_ref, s32[384,8192]{1,0:T(8,128)} %counts_hbm.1, s32[64,128]{1,0:T(8,128)} %bitcast.6), custom_call_target="tpu_custom_call" | custom-call | tf_op jit(solution)/shard_map/sketch/pallas_call | solution.py:147
  12.6 21.5 %all_to_all.10.pieces_ref = bf16[32,32,128]{2,1,0:T(8,128)(2,1)S(1)} all-to-all(bf16[32,32,128]{2,1,0:T(8,128)(2,1)S(1)} %get-tuple-element.27), channel_id=1, replica_groups=mesh['x'=4,'core'=2,'y'=4,'z'=8] {'y','z'}, dimensions={0} | all-to-all | bytes 524288 | tf_op jit(solution)/shard_map/all_to_all | solution.py:447
  34.2 15.8 %all_to_all.11.g_ref = bf16[32,32,128]{2,1,0:T(8,128)(2,1)S(1)} all-to-all(bf16[32,32,128]{2,1,0:T(8,128)(2,1)S(1)} %share.1), channel_id=1, replica_groups=mesh['x'=4,'core'=2,'y'=4,'z'=8] {'y','z'}, dimensions={0} | all-to-all | bytes 524288 | tf_op jit(solution)/shard_map/all_to_all | solution.py:448
  50.0 0.7 gram.1
  50.7 3.7 %collective-permute-start = (f32[240,128]{1,0:T(8,128)S(1)}, f32[240,128]{1,0:T(8,128)S(1)}, u32[]{:S(2)}, u32[]{:S(2)}) collective-permute-start(f32[240,128]{1,0:T(8,128)S(1)} %slice_bitcast_fusion), channel_id=1, source_target_pairs={{0,32},{32,0},{1,33},{33,1},{2,34},{34,2},{3,35},{35,3},{4,36},{36... | collective-permute-start | bytes 368648 | tf_op jit(solution)/shard_map/ppermute | solution.py:429
  54.4 1.0 collective-permute-done
  55.4 2.6 %collective-permute-start.3 = (f32[240,128]{1,0:T(8,128)S(1)}, f32[240,128]{1,0:T(8,128)S(1)}, u32[]{:S(2)}, u32[]{:S(2)}) collective-permute-start(f32[240,128]{1,0:T(8,128)S(1)} %bitcast_add_fusion), channel_id=1, source_target_pairs={{0,192},{64,0},{128,64},{192,128},{1,193},{65,1},{129,65},{193,129... | collective-permute-start | bytes 368648 | tf_op jit(solution)/shard_map/ppermute | solution.py:433
  58.0 1.7 %collective-permute-start.1 = (f32[240,128]{1,0:T(8,128)S(1)}, f32[240,128]{1,0:T(8,128)S(1)}, u32[]{:S(2)}, u32[]{:S(2)}) collective-permute-start(f32[240,128]{1,0:T(8,128)S(1)} %bitcast_add_fusion), channel_id=1, source_target_pairs={{0,128},{64,192},{128,0},{192,64},{1,129},{65,193},{129,1},{193,65... | collective-permute-start | bytes 368648 | tf_op jit(solution)/shard_map/ppermute | solution.py:433
  59.7 0.6 collective-permute-done.3
  60.3 4.5 %collective-permute-done.2 = f32[240,128]{1,0:T(8,128)S(1)} collective-permute-done((f32[240,128]{1,0:T(8,128)S(1)}, f32[240,128]{1,0:T(8,128)S(1)}, u32[]{:S(2)}, u32[]{:S(2)}) %collective-permute-start.2) | collective-permute-done | bytes 122912 | tf_op jit(solution)/shard_map/ppermute | solution.py:433
  65.1 2.5 %collective-permute-start.4 = (f32[240,128]{1,0:T(8,128)S(1)}, f32[240,128]{1,0:T(8,128)S(1)}, u32[]{:S(2)}, u32[]{:S(2)}) collective-permute-start(f32[240,128]{1,0:T(8,128)S(1)} %add_add_fusion.mine_ref), channel_id=1, source_target_pairs={{0,32},{32,0},{1,33},{33,1},{2,34},{34,2},{3,35},{35,3},{4,36},{36... | collective-permute-start | bytes 368648 | tf_op jit(solution)/shard_map/ppermute | solution.py:429
  67.7 1.0 collective-permute-done.4.theirs_ref
  68.7 7.2 %basis.1 = (f32[256,256]{1,0:T(8,128)S(1)}, f32[384,256]{1,0:T(8,128)S(1)}, bf16[4,2,32,384]{3,2,1,0:T(8,128)(2,1)S(1)}, bf16[400,8192]{1,0:T(8,128)(2,1)S(1)}) custom-call(f32[240,128]{1,0:T(8,128)S(1)} %add_add_fusion.mine_ref, f32[240,128]{1,0:T(8,128)S(1)} %collective-permute-done.4.theirs_ref, f32[384,256]{1,0:T(8,128)S(1)} %get-tuple-element.30.own_ref, ...), custom_call_target="tpu_custom_call" | custom-call | tf_op jit(solution)/shard_map/basis/pallas_call | solution.py:359
  75.8 1.8 %project.2 = (bf16[32,4096]{1,0:T(8,128)(2,1)S(1)}, bf16[32,4096]{1,0:T(8,128)(2,1)S(1)}, bf16[32,4096]{1,0:T(8,128)(2,1)S(1)}, bf16[32,4096]{1,0:T(8,128)(2,1)S...) custom-call(bf16[4,2,32,384]{3,2,1,0:T(8,128)(2,1)S(1)} %get-tuple-e, ...), custom_call_target="tpu_custom_call" | custom-call | tf_op jit(solution)/shard_map/project/pallas_call | solution.py:418
  77.7 0.5 collective-permute-start.8
  78.3 0.4 collective-permute-start.5
  78.8 0.5 collective-permute-done.8
  79.7 2.5 %collective-permute-start.12 = (bf16[32,4096]{1,0:T(8,128)(2,1)S(1)}, bf16[32,4096]{1,0:T(8,128)(2,1)S(1)}, u32[]{:S(2)}, u32[]{:S(2)}) collective-permute-start(bf16[32,4096]{1,0:T(8,128)(2,1)S(1)} %add_convert_fusion.1), channel_id=1, source_target_pairs={{0,192},{64,0},{128,64},{192,128},{1,193},{65,1},{129,65},{193,129... | collective-permute-start | bytes 786440 | tf_op jit(solution)/shard_map/ppermute | solution.py:433
  82.4 5.8 %collective-permute-done.9 = bf16[32,4096]{1,0:T(8,128)(2,1)S(1)} collective-permute-done((bf16[32,4096]{1,0:T(8,128)(2,1)S(1)}, bf16[32,4096]{1,0:T(8,128)(2,1)S(1)}, u32[]{:S(2)}, u32[]{:S(2)}) %collective-permute-start.9) | collective-permute-done | bytes 262176 | tf_op jit(solution)/shard_map/ppermute | solution.py:433
  88.6 2.9 %collective-permute-start.13 = (bf16[32,8192]{1,0:T(8,128)(2,1)S(1)}, bf16[32,8192]{1,0:T(8,128)(2,1)S(1)}, u32[]{:S(2)}, u32[]{:S(2)}) collective-permute-start(bf16[32,8192]{1,0:T(8,128)(2,1)S(1)} %pad_maximum_fusion.1), channel_id=1, source_target_pairs={{0,192},{64,0},{128,64},{192,128},{1,193},{65,1},{129,65},{193,129... | collective-permute-start | bytes 1572872 | tf_op jit(solution)/shard_map/ppermute | solution.py:433
  91.6 2.0 %project.3 = (bf16[32,8192]{1,0:T(8,128)(2,1)S(1)}, bf16[32,8192]{1,0:T(8,128)(2,1)S(1)}, f32[384,256]{1,0:T(8,128)}, f32[64,128]{1,0:T(8,128)}) custom-call(f32[384,256]{1,0:T(8,128)S(1)} %get-tuple-element.32.own_ref, f32[256,256]{1,0:T(8,128)S(1)} %get-tuple-element.33.inverse_ref, bf16[4,2,32,384]{3,2,1,0:T(8,128)(2,1)S(1)} %get-tuple-element.40.bt_ref, ...), custom_call_target="tpu_custom_call" | custom-call | tf_op jit(solution)/shard_map/project/pallas_call | solution.py:418
  93.5 1.8 %collective-permute-start.7 = (bf16[32,8192]{1,0:T(8,128)(2,1)S(1)}, bf16[32,8192]{1,0:T(8,128)(2,1)S(1)}, u32[]{:S(2)}, u32[]{:S(2)}) collective-permute-start(bf16[32,8192]{1,0:T(8,128)(2,1)S(1)} %get-tuple-element.43), channel_id=1, source_target_pairs={{0,32},{32,0},{1,33},{33,1},{2,34},{34,2},{3,35},{35,3},{4,36},{36... | collective-permute-start | bytes 1572872 | tf_op jit(solution)/shard_map/ppermute | solution.py:429
  95.3 6.5 %collective-permute-done.10 = bf16[32,8192]{1,0:T(8,128)(2,1)S(1)} collective-permute-done((bf16[32,8192]{1,0:T(8,128)(2,1)S(1)}, bf16[32,8192]{1,0:T(8,128)(2,1)S(1)}, u32[]{:S(2)}, u32[]{:S(2)}) %collective-permute-start.10) | collective-permute-done | bytes 524320 | tf_op jit(solution)/shard_map/ppermute | solution.py:433
  101.8 1.1 %add_convert_fusion = bf16[32,8192]{1,0:T(8,128)(2,1)} fusion(bf16[32,8192]{1,0:T(8,128)(2,1)S(1)} %collective-permute-done.13, bf16[32,8192]{1,0:T(8,128)(2,1)S(1)} %collective-permute-done.10, bf16[32,8192]{1,0:T(8,128)(2,1)S(1)} %collective-permute-done.7, bf16[32,8192]{1,0:T(8,128)(2,1)S(1)} %get-tuple-element.42), kind=kLoop, calls=%fused_computation | loop fusion | flops 2097152 | bytes 2621440 | tf_op jit(solution)/shard_map/convert_element_type | solution.py:478
  (26 shorter events, 1.7 us)
Async XLA Ops:
  50.7 4.7 %collective-permute-start = (f32[240,128]{1,0:T(8,128)S(1)}, f32[240,128]{1,0:T(8,128)S(1)}, u32[]{:S(2)}, u32[]{:S(2)}) collective-permute-start(f32[240,128]{1,0:T(8,128)S(1)} %slice_bitcast_fusion), channel_id=1, source_target_pairs={{0,32},{32,0},{1,33},{33,1},{2,34},{34,2},{3,35},{35,3},{4,36},{36... | collective-permute-start | bytes 368648 | tf_op jit(solution)/shard_map/ppermute | solution.py:429
  55.4 4.9 %collective-permute-start.3 = (f32[240,128]{1,0:T(8,128)S(1)}, f32[240,128]{1,0:T(8,128)S(1)}, u32[]{:S(2)}, u32[]{:S(2)}) collective-permute-start(f32[240,128]{1,0:T(8,128)S(1)} %bitcast_add_fusion), channel_id=1, source_target_pairs={{0,192},{64,0},{128,64},{192,128},{1,193},{65,1},{129,65},{193,129... | collective-permute-start | bytes 368648 | tf_op jit(solution)/shard_map/ppermute | solution.py:433
  58.0 6.8 %collective-permute-start.2 = (f32[240,128]{1,0:T(8,128)S(1)}, f32[240,128]{1,0:T(8,128)S(1)}, u32[]{:S(2)}, u32[]{:S(2)}) collective-permute-start(f32[240,128]{1,0:T(8,128)S(1)} %bitcast_add_fusion), channel_id=1, source_target_pairs={{0,64},{64,128},{128,192},{192,0},{1,65},{65,129},{129,193},{193,1... | collective-permute-start | bytes 368648 | tf_op jit(solution)/shard_map/ppermute | solution.py:433
  58.0 7.1 %collective-permute-start.1 = (f32[240,128]{1,0:T(8,128)S(1)}, f32[240,128]{1,0:T(8,128)S(1)}, u32[]{:S(2)}, u32[]{:S(2)}) collective-permute-start(f32[240,128]{1,0:T(8,128)S(1)} %bitcast_add_fusion), channel_id=1, source_target_pairs={{0,128},{64,192},{128,0},{192,64},{1,129},{65,193},{129,1},{193,65... | collective-permute-start | bytes 368648 | tf_op jit(solution)/shard_map/ppermute | solution.py:433
  65.1 3.5 %collective-permute-start.4 = (f32[240,128]{1,0:T(8,128)S(1)}, f32[240,128]{1,0:T(8,128)S(1)}, u32[]{:S(2)}, u32[]{:S(2)}) collective-permute-start(f32[240,128]{1,0:T(8,128)S(1)} %add_add_fusion.mine_ref), channel_id=1, source_target_pairs={{0,32},{32,0},{1,33},{33,1},{2,34},{34,2},{3,35},{35,3},{4,36},{36... | collective-permute-start | bytes 368648 | tf_op jit(solution)/shard_map/ppermute | solution.py:429
  77.7 1.6 %collective-permute-start.8 = (bf16[32,4096]{1,0:T(8,128)(2,1)S(1)}, bf16[32,4096]{1,0:T(8,128)(2,1)S(1)}, u32[]{:S(2)}, u32[]{:S(2)}) collective-permute-start(bf16[32,4096]{1,0:T(8,128)(2,1)S(1)} %get-tuple-element.46), channel_id=1, source_target_pairs={{0,32},{32,0},{1,33},{33,1},{2,34},{34,2},{3,35},{35,3},{4,36},{36... | collective-permute-start | bytes 786440 | tf_op jit(solution)/shard_map/ppermute | solution.py:429
  78.1 1.5 %collective-permute-start.11 = (bf16[32,4096]{1,0:T(8,128)(2,1)S(1)}, bf16[32,4096]{1,0:T(8,128)(2,1)S(1)}, u32[]{:S(2)}, u32[]{:S(2)}) collective-permute-start(bf16[32,4096]{1,0:T(8,128)(2,1)S(1)} %get-tuple-element.49), channel_id=1, source_target_pairs={{0,32},{32,0},{1,33},{33,1},{2,34},{34,2},{3,35},{35,3},{4,36},{36... | collective-permute-start | bytes 786440 | tf_op jit(solution)/shard_map/ppermute | solution.py:429
  78.3 4.0 %collective-permute-start.5 = (bf16[32,8192]{1,0:T(8,128)(2,1)S(1)}, bf16[32,8192]{1,0:T(8,128)(2,1)S(1)}, u32[]{:S(2)}, u32[]{:S(2)}) collective-permute-start(bf16[32,8192]{1,0:T(8,128)(2,1)S(1)} %get-tuple-element.38), channel_id=1, source_target_pairs={{0,32},{32,0},{1,33},{33,1},{2,34},{34,2},{3,35},{35,3},{4,36},{36... | collective-permute-start | bytes 1572872 | tf_op jit(solution)/shard_map/ppermute | solution.py:429
  78.6 9.7 %collective-permute-start.6 = (bf16[32,8192]{1,0:T(8,128)(2,1)S(1)}, bf16[32,8192]{1,0:T(8,128)(2,1)S(1)}, u32[]{:S(2)}, u32[]{:S(2)}) collective-permute-start(bf16[32,8192]{1,0:T(8,128)(2,1)S(1)} %get-tuple-element.39), channel_id=1, source_target_pairs={{0,32},{32,0},{1,33},{33,1},{2,34},{34,2},{3,35},{35,3},{4,36},{36... | collective-permute-start | bytes 1572872 | tf_op jit(solution)/shard_map/ppermute | solution.py:429
  79.3 8.8 %collective-permute-start.9 = (bf16[32,4096]{1,0:T(8,128)(2,1)S(1)}, bf16[32,4096]{1,0:T(8,128)(2,1)S(1)}, u32[]{:S(2)}, u32[]{:S(2)}) collective-permute-start(bf16[32,4096]{1,0:T(8,128)(2,1)S(1)} %add_convert_fusion.2), channel_id=1, source_target_pairs={{0,64},{64,128},{128,192},{192,0},{1,65},{65,129},{129,193},{193,1... | collective-permute-start | bytes 786440 | tf_op jit(solution)/shard_map/ppermute | solution.py:433
  79.7 8.8 %collective-permute-start.12 = (bf16[32,4096]{1,0:T(8,128)(2,1)S(1)}, bf16[32,4096]{1,0:T(8,128)(2,1)S(1)}, u32[]{:S(2)}, u32[]{:S(2)}) collective-permute-start(bf16[32,4096]{1,0:T(8,128)(2,1)S(1)} %add_convert_fusion.1), channel_id=1, source_target_pairs={{0,192},{64,0},{128,64},{192,128},{1,193},{65,1},{129,65},{193,129... | collective-permute-start | bytes 786440 | tf_op jit(solution)/shard_map/ppermute | solution.py:433
  88.3 13.5 %collective-permute-start.10 = (bf16[32,8192]{1,0:T(8,128)(2,1)S(1)}, bf16[32,8192]{1,0:T(8,128)(2,1)S(1)}, u32[]{:S(2)}, u32[]{:S(2)}) collective-permute-start(bf16[32,8192]{1,0:T(8,128)(2,1)S(1)} %pad_maximum_fusion), channel_id=1, source_target_pairs={{0,64},{64,128},{128,192},{192,0},{1,65},{65,129},{129,193},{193,1... | collective-permute-start | bytes 1572872 | tf_op jit(solution)/shard_map/ppermute | solution.py:433
  88.6 13.2 %collective-permute-start.13 = (bf16[32,8192]{1,0:T(8,128)(2,1)S(1)}, bf16[32,8192]{1,0:T(8,128)(2,1)S(1)}, u32[]{:S(2)}, u32[]{:S(2)}) collective-permute-start(bf16[32,8192]{1,0:T(8,128)(2,1)S(1)} %pad_maximum_fusion.1), channel_id=1, source_target_pairs={{0,192},{64,0},{128,64},{192,128},{1,193},{65,1},{129,65},{193,129... | collective-permute-start | bytes 1572872 | tf_op jit(solution)/shard_map/ppermute | solution.py:433
  93.5 8.2 %collective-permute-start.7 = (bf16[32,8192]{1,0:T(8,128)(2,1)S(1)}, bf16[32,8192]{1,0:T(8,128)(2,1)S(1)}, u32[]{:S(2)}, u32[]{:S(2)}) collective-permute-start(bf16[32,8192]{1,0:T(8,128)(2,1)S(1)} %get-tuple-element.43), channel_id=1, source_target_pairs={{0,32},{32,0},{1,33},{33,1},{2,34},{34,2},{3,35},{35,3},{4,36},{36... | collective-permute-start | bytes 1572872 | tf_op jit(solution)/shard_map/ppermute | solution.py:429

commit v4 on v3

--- a/solution.py
+++ b/solution.py
@@ -22,7 +22,7 @@
 PIVOTS = 32
 TAIL = 16
 MEAN_ROWS = 8
-TRIANGLE = 192
+TRIANGLE = 160
 MEANS = 16
 
 
@@ -193,6 +193,18 @@
     )(pieces)
 
 
+def fold(block):
+    right = lax.broadcasted_iota(I32, (32, LANES), 1) >= 64
+    return jnp.concatenate([block[:64], jnp.where(right, block[64:96], pltpu.roll(block[96:], 64, 1))], axis=0)
+
+
+def unfold(rows):
+    right = lax.broadcasted_iota(I32, (32, LANES), 1) >= 64
+    folded = rows[64:96]
+    upper, lower = jnp.where(right, folded, 0.0), jnp.where(right, pltpu.roll(folded, 64, 1), 0.0)
+    return jnp.concatenate([rows[:64], upper, lower], axis=0)
+
+
 def gram_kernel(g_ref, lsum_ref, pay_ref, own_ref):
     my_x, my_core = lax.axis_index("x"), lax.axis_index("core")
     parts, held, _ = g_ref.shape
@@ -214,8 +226,8 @@
     sums = lsum_ref.shape[0] // 2
     for half in range(2):
         at = my_core ^ half
-        pay_ref[at, :LANES] = gram[LANES * half : LANES * (half + 1), LANES * half : LANES * (half + 1)]
-        pay_ref[at, LANES:TRIANGLE] = gram[64 * half : 64 * (half + 1), LANES:]
+        pay_ref[at, :96] = fold(gram[LANES * half : LANES * (half + 1), LANES * half : LANES * (half + 1)])
+        pay_ref[at, 96:TRIANGLE] = gram[64 * half : 64 * (half + 1), LANES:]
         pay_ref[at, TRIANGLE : TRIANGLE + MEANS] = means
         pay_ref[at, TRIANGLE + MEANS :] = lsum_ref[sums * half : sums * (half + 1)]
 
@@ -313,10 +325,10 @@
         apart = jnp.concatenate(apart, axis=0)
         docs = own_ref.shape[0]
         shift = over_rows(*stacked(jnp.concatenate([apart, jnp.zeros_like(apart)], axis=0))) * jnp.float32(docs)
-        work[:LANES, :LANES] = first[:LANES] + shift[:LANES, :LANES]
-        work[:64, LANES:] = first[LANES:TRIANGLE] + shift[:64, LANES:]
-        work[64:LANES, LANES:] = second[LANES:TRIANGLE] + shift[64:LANES, LANES:]
-        work[LANES:, LANES:] = second[:LANES] + shift[LANES:, LANES:]
+        work[:LANES, :LANES] = unfold(first) + shift[:LANES, :LANES]
+        work[:64, LANES:] = first[96:TRIANGLE] + shift[:64, LANES:]
+        work[64:LANES, LANES:] = second[96:TRIANGLE] + shift[64:LANES, LANES:]
+        work[LANES:, LANES:] = unfold(second) + shift[LANES:, LANES:]
         work[LANES:, :LANES] = jnp.zeros((LANES, LANES), F32)
         mean_at = lax.broadcasted_iota(I32, (8, SKETCH), 0) == 2 * my_x + my_core
         own_shift = jnp.sum(jnp.where(mean_at, apart, 0.0), axis=0, keepdims=True)
@@ -380,10 +392,10 @@
     return jnp.concatenate([low, high], axis=0) * (1.0 / docs)
 
 
-def project_kernel(bt_ref, w_ref, centre_ref, idf_ref, mine_ref, theirs_ref, *out_refs, first, pieces, cut):
+def project_kernel(bt_ref, w_ref, centre_ref, idf_ref, mine_ref, theirs_ref, *out_refs, pieces):
     _, cores, rows, depth = bt_ref.shape
     width = w_ref.shape[1]
-    left = bt_ref[first : first + pieces].reshape(pieces * cores * rows, depth)
+    left = bt_ref[:pieces].reshape(pieces * cores * rows, depth)
     sums = jnp.sum(left.astype(F32), axis=1, keepdims=True)
     apart = idf_ref[...] * (centre_ref[...] - log_means(mine_ref, theirs_ref, 8 * depth))
     block = 512
@@ -394,23 +406,17 @@
         product = (product + sums * shift).astype(BF16)
         for k in range(pieces * cores):
             value = product[k * rows : (k + 1) * rows]
-            if not cut:
-                out_refs[k][:, at : at + block] = value
-            elif k >= cores:
+            if k >= cores:
                 out_refs[cores + k][:, at : at + block] = value
             else:
                 begin = at % (width // 2)
                 out_refs[2 * (2 * at // width) + k][:, begin : begin + block] = value
 
 
-def project_last_kernel(own_ref, inverse_ref, bt_ref, w_ref, centre_ref, idf_ref, mine_ref, theirs_ref, *out_refs):
-    q_ref, mean_ref = out_refs[2:]
+def finish_kernel(own_ref, inverse_ref, idf_ref, mine_ref, theirs_ref, q_ref, mean_ref):
     q_ref[...] = by_rows(own_ref[...], inverse_ref[...])
     docs = 8 * own_ref.shape[0]
     mean_ref[...] = idf_ref[...] * (1.0 + log_means(mine_ref, theirs_ref, docs))
-    project_kernel(
-        bt_ref, w_ref, centre_ref, idf_ref, mine_ref, theirs_ref, *out_refs[:2], first=3, pieces=1, cut=False
-    )
 
 
 def project_call(kernel, outs, operands):
@@ -433,6 +439,10 @@
     return lax.ppermute(value, "x", [(i, (i + by) % 4) for i in range(4)])
 
 
+def three_sum(a, b, c):
+    return (a.astype(F32) + b.astype(F32) + c.astype(F32)).astype(BF16)
+
+
 def half_sum(a, b):
     return (a.astype(F32) + b.astype(F32)).astype(BF16)
 
@@ -456,25 +466,28 @@
     half = cols // 2
     narrow, wide = (jax.ShapeDtypeStruct((SKETCH // 8, n), BF16) for n in (half, cols))
     rest = (weighted, centres, idf, mine, theirs)
-    ours2a, other2a, ours2b, other2b, ours1, other1, ours3, other3 = project_call(
-        functools.partial(project_kernel, first=0, pieces=3, cut=True), [narrow] * 4 + [wide] * 4, (flipped,) + rest
+    ours2a, other2a, ours2b, other2b, ours1, other1, ours3, other3, ours0, other0 = project_call(
+        functools.partial(project_kernel, pieces=4), [narrow] * 4 + [wide] * 6, (flipped,) + rest
     )
     relay_up = shift_x(half_sum(ours2a, swap(other2a)), 1)
     relay_down = shift_x(half_sum(ours2b, swap(other2b)), -1)
     theirs1, theirs3 = swap(other1), swap(other3)
-    up = ours1.astype(F32) + theirs1.astype(F32)
-    up = jnp.concatenate([up[:, :half] + relay_up.astype(F32), up[:, half:]], axis=1).astype(BF16)
-    down = ours3.astype(F32) + theirs3.astype(F32)
-    down = jnp.concatenate([down[:, :half], down[:, half:] + relay_down.astype(F32)], axis=1).astype(BF16)
-    from_below, from_above = shift_x(up, 1), shift_x(down, -1)
-    flipped, _, _ = lax.optimization_barrier((flipped, theirs1, theirs3))
-    ours0, other0, basis, means = project_call(
-        project_last_kernel,
-        [wide, wide, jax.ShapeDtypeStruct(own.shape, F32), jax.ShapeDtypeStruct(idf.shape, F32)],
-        (own, inverse, flipped) + rest,
+    near_up = half_sum(ours1[:, half:], theirs1[:, half:])
+    near_down = half_sum(ours3[:, :half], theirs3[:, :half])
+    theirs1, theirs3, near_up, near_down = lax.optimization_barrier((theirs1, theirs3, near_up, near_down))
+    below_b, above_a = shift_x(near_up, 1), shift_x(near_down, -1)
+    below_a = shift_x(three_sum(ours1[:, :half], theirs1[:, :half], relay_up), 1)
+    above_b = shift_x(three_sum(ours3[:, half:], theirs3[:, half:], relay_down), -1)
+    own, _, _ = lax.optimization_barrier((own, theirs1, theirs3))
+    basis, means = project_call(
+        finish_kernel,
+        [jax.ShapeDtypeStruct(own.shape, F32), jax.ShapeDtypeStruct(idf.shape, F32)],
+        (own, inverse, idf, mine, theirs),
     )
     total = ours0.astype(F32) + swap(other0).astype(F32)
-    total = total + from_below.astype(F32) + from_above.astype(F32)
+    below = jnp.concatenate([below_a, below_b], axis=1).astype(F32)
+    above = jnp.concatenate([above_a, above_b], axis=1).astype(F32)
+    total = total + below + above
     return (basis, total.astype(BF16), means.reshape(cols))
 
 

time: 104 us -> 101 us (0.971)
  waiting for transfers between devices: 20.3 us -> 18.1 us
    ppermute x7, starting transfers between devices: 9.09 us -> 6.34 us  [swap(): return lax.ppermute(value, 'core', [(0, 1), (1, 0)])]
    ppermute x7 -> x9, starting transfers between devices: 9.93 us -> 12.7 us  [shift_x(): return lax.ppermute(value, 'x', [(i, (i + by) % 4) for i in range(4)])]
    ppermute x7 -> x9, waiting for transfers between devices: 17.6 us -> 15.8 us  [shift_x(): return lax.ppermute(value, 'x', [(i, (i + by) % 4) for i in range(4)])]
  transfers between devices with their start and end apart: 14 -> 16, of which waited for: 9 -> 9; matrix products, arithmetic and copies ran while one was open for 1% -> 0% of each run, Pallas kernels for 2% -> 1%
where the time goes in v4:
time: 101 us; the launch traced here: 100 us
  blocking collectives  37.3 us (37%)
  Pallas kernels  23.1 us (23%)
  starting transfers between devices  19 us (19%)
  waiting for transfers between devices  18.1 us (18%)
  other arithmetic  1.54 us (2%)
  between operations  1.4 us (1%)
    all_to_all x1, blocking collectives, body(): pieces = lax.all_to_all(sketch_part, terms_axes, 0, 0)  21.5 us
    ppermute x9, waiting for transfers between devices, shift_x(): return lax.ppermute(value, 'x', [(i, (i + by) % 4) for i in range(4)])  15.8 us
    all_to_all x1, blocking collectives, body(): gathered = lax.all_to_all(share_call(pieces), terms_axes, 0, 0)  15.8 us
    ppermute x9, starting transfers between devices, shift_x(): return lax.ppermute(value, 'x', [(i, (i + by) % 4) for i in range(4)])  12.7 us
    pallas_call x1, Pallas kernels, sketch_call(): pl.pallas_call(sketch_kernel, in_specs=[pl.BlockSpec(memory_space=pltpu.S...  11.4 us
    pallas_call x1, Pallas kernels, basis_call(): pl.pallas_call(basis_kernel, in_specs=[in_vmem] * 3 + [in_hbm], out_specs...  7.23 us
    ppermute x7, starting transfers between devices, swap(): return lax.ppermute(value, 'core', [(0, 1), (1, 0)])  6.34 us
    pallas_call x2, Pallas kernels, project_call(): pl.pallas_call(kernel, in_specs=[in_vmem] * len(operands), out_specs=[in_...  3.64 us
  transfers between devices with their start and end apart: 16, of which 9 were waited for; matrix products, arithmetic and copies ran while one was open for 0% of the time, Pallas kernels for 1%

profile of v4, /device:TPU:1, one launch (start us, length us, event | category | flops | bytes accessed | tf_op | source)
XLA Modules:
  0.0 100.4 jit_solution(100667199795265592)
XLA Ops:
  1.3 11.4 %sketch.1 = (bf16[32,32,128]{2,1,0:T(8,128)(2,1)S(1)}, bf16[400,8192]{1,0:T(8,128)(2,1)}, f32[64,128]{1,0:T(8,128)S(1)}, f32[64,128]{1,0:T(8,128)S(1)}, f32[64,128]{1,0:T(8,128)S(1)}) custom-call(s32[1]{0:T(128)S(6)} %copy.6.seed_ref, s32[384,8192]{1,0:T(8,128)} %counts_hbm.1, s32[64,128]{1,0:T(8,128)} %bitcast.6), custom_call_target="tpu_custom_call" | custom-call | tf_op jit(solution)/shard_map/sketch/pallas_call | solution.py:147
  12.6 21.5 %all_to_all.10.pieces_ref = bf16[32,32,128]{2,1,0:T(8,128)(2,1)S(1)} all-to-all(bf16[32,32,128]{2,1,0:T(8,128)(2,1)S(1)} %get-tuple-element.31), channel_id=1, replica_groups=mesh['x'=4,'core'=2,'y'=4,'z'=8] {'y','z'}, dimensions={0} | all-to-all | bytes 524288 | tf_op jit(solution)/shard_map/all_to_all | solution.py:457
  34.2 15.8 %all_to_all.11.g_ref = bf16[32,32,128]{2,1,0:T(8,128)(2,1)S(1)} all-to-all(bf16[32,32,128]{2,1,0:T(8,128)(2,1)S(1)} %share.1), channel_id=1, replica_groups=mesh['x'=4,'core'=2,'y'=4,'z'=8] {'y','z'}, dimensions={0} | all-to-all | bytes 524288 | tf_op jit(solution)/shard_map/all_to_all | solution.py:458
  50.0 0.8 gram.1
  50.8 3.7 %collective-permute-start = (f32[208,128]{1,0:T(8,128)S(1)}, f32[208,128]{1,0:T(8,128)S(1)}, u32[]{:S(2)}, u32[]{:S(2)}) collective-permute-start(f32[208,128]{1,0:T(8,128)S(1)} %slice_bitcast_fusion), channel_id=1, source_target_pairs={{0,32},{32,0},{1,33},{33,1},{2,34},{34,2},{3,35},{35,3},{4,36},{36... | collective-permute-start | bytes 319496 | tf_op jit(solution)/shard_map/ppermute | solution.py:435
  54.5 1.0 collective-permute-done
  55.4 2.6 %collective-permute-start.3 = (f32[208,128]{1,0:T(8,128)S(1)}, f32[208,128]{1,0:T(8,128)S(1)}, u32[]{:S(2)}, u32[]{:S(2)}) collective-permute-start(f32[208,128]{1,0:T(8,128)S(1)} %bitcast_add_fusion), channel_id=1, source_target_pairs={{0,192},{64,0},{128,64},{192,128},{1,193},{65,1},{129,65},{193,129... | collective-permute-start | bytes 319496 | tf_op jit(solution)/shard_map/ppermute | solution.py:439
  58.0 1.7 %collective-permute-start.1 = (f32[208,128]{1,0:T(8,128)S(1)}, f32[208,128]{1,0:T(8,128)S(1)}, u32[]{:S(2)}, u32[]{:S(2)}) collective-permute-start(f32[208,128]{1,0:T(8,128)S(1)} %bitcast_add_fusion), channel_id=1, source_target_pairs={{0,128},{64,192},{128,0},{192,64},{1,129},{65,193},{129,1},{193,65... | collective-permute-start | bytes 319496 | tf_op jit(solution)/shard_map/ppermute | solution.py:439
  60.0 5.8 %collective-permute-done.2 = f32[208,128]{1,0:T(8,128)S(1)} collective-permute-done((f32[208,128]{1,0:T(8,128)S(1)}, f32[208,128]{1,0:T(8,128)S(1)}, u32[]{:S(2)}, u32[]{:S(2)}) %collective-permute-start.2) | collective-permute-done | bytes 106528 | tf_op jit(solution)/shard_map/ppermute | solution.py:439
  65.8 1.2 %collective-permute-start.4 = (f32[208,128]{1,0:T(8,128)S(1)}, f32[208,128]{1,0:T(8,128)S(1)}, u32[]{:S(2)}, u32[]{:S(2)}) collective-permute-start(f32[208,128]{1,0:T(8,128)S(1)} %add_add_fusion.mine_ref), channel_id=1, source_target_pairs={{0,32},{32,0},{1,33},{33,1},{2,34},{34,2},{3,35},{35,3},{4,36},{36... | collective-permute-start | bytes 319496 | tf_op jit(solution)/shard_map/ppermute | solution.py:435
  67.0 1.0 collective-permute-done.4.theirs_ref
  68.0 7.2 %basis.1 = (f32[256,256]{1,0:T(8,128)S(1)}, f32[384,256]{1,0:T(8,128)S(1)}, bf16[4,2,32,384]{3,2,1,0:T(8,128)(2,1)S(1)}, bf16[400,8192]{1,0:T(8,128)(2,1)S(1)}) custom-call(f32[208,128]{1,0:T(8,128)S(1)} %add_add_fusion.mine_ref, f32[208,128]{1,0:T(8,128)S(1)} %collective-permute-done.4.theirs_ref, f32[384,256]{1,0:T(8,128)S(1)} %get-tuple-element.34.own_ref, ...), custom_call_target="tpu_custom_call" | custom-call | tf_op jit(solution)/shard_map/basis/pallas_call | solution.py:371
  75.2 2.4 %project.2 = (bf16[32,4096]{1,0:T(8,128)(2,1)S(1)}, bf16[32,4096]{1,0:T(8,128)(2,1)S(1)}, bf16[32,4096]{1,0:T(8,128)(2,1)S(1)}, bf16[32,4096]{1,0:T(8,128)(2,1)S...) custom-call(bf16[4,2,32,384]{3,2,1,0:T(8,128)(2,1)S(1)} %get-tuple-e, ...), custom_call_target="tpu_custom_call" | custom-call | tf_op jit(solution)/shard_map/project/pallas_call | solution.py:424
  77.6 0.4 collective-permute-start.8
  78.2 0.4 collective-permute-start.5
  78.7 0.4 collective-permute-start.7
  79.6 2.5 %collective-permute-start.14 = (bf16[32,4096]{1,0:T(8,128)(2,1)S(1)}, bf16[32,4096]{1,0:T(8,128)(2,1)S(1)}, u32[]{:S(2)}, u32[]{:S(2)}) collective-permute-start(bf16[32,4096]{1,0:T(8,128)(2,1)S(1)} %add_convert_fusion.2), channel_id=1, source_target_pairs={{0,192},{64,0},{128,64},{192,128},{1,193},{65,1},{129,65},{193,129... | collective-permute-start | bytes 786440 | tf_op jit(solution)/shard_map/ppermute | solution.py:439
  82.6 2.7 %collective-permute-start.12 = (bf16[32,4096]{1,0:T(8,128)(2,1)S(1)}, bf16[32,4096]{1,0:T(8,128)(2,1)S(1)}, u32[]{:S(2)}, u32[]{:S(2)}) collective-permute-start(bf16[32,4096]{1,0:T(8,128)(2,1)S(1)} %add_convert_fusion.5), channel_id=1, source_target_pairs={{0,192},{64,0},{128,64},{192,128},{1,193},{65,1},{129,65},{193,129... | collective-permute-start | bytes 786440 | tf_op jit(solution)/shard_map/ppermute | solution.py:439
  85.3 2.8 %collective-permute-done.9 = bf16[32,4096]{1,0:T(8,128)(2,1)S(1)} collective-permute-done((bf16[32,4096]{1,0:T(8,128)(2,1)S(1)}, bf16[32,4096]{1,0:T(8,128)(2,1)S(1)}, u32[]{:S(2)}, u32[]{:S(2)}) %collective-permute-start.9) | collective-permute-done | bytes 262176 | tf_op jit(solution)/shard_map/ppermute | solution.py:439
  88.4 2.7 %collective-permute-start.15 = (bf16[32,4096]{1,0:T(8,128)(2,1)S(1)}, bf16[32,4096]{1,0:T(8,128)(2,1)S(1)}, u32[]{:S(2)}, u32[]{:S(2)}) collective-permute-start(bf16[32,4096]{1,0:T(8,128)(2,1)S(1)} %add_convert_fusion.1), channel_id=1, source_target_pairs={{0,192},{64,0},{128,64},{192,128},{1,193},{65,1},{129,65},{193,129... | collective-permute-start | bytes 786440 | tf_op jit(solution)/shard_map/ppermute | solution.py:439
  91.1 1.3 %project.3 = (f32[384,256]{1,0:T(8,128)}, f32[64,128]{1,0:T(8,128)}) custom-call(f32[384,256]{1,0:T(8,128)S(1)} %get-tuple-element.47.own_ref, f32[256,256]{1,0:T(8,128)S(1)} %get-tuple-element.48.inverse_ref, f32[64,128]{1,0:T(8,128)S(1)} %get-tuple-element.40.idf_ref, f32[208,128]{1,0:T(8,128)S(1)} %add_add_fusion.mine_ref, ...), custom_call_target="tpu_custom_call" | custom-call | tf_op jit(solution)/shard_map/project/pallas_call | solution.py:424
  92.4 1.3 %collective-permute-done.11 = bf16[32,4096]{1,0:T(8,128)(2,1)S(1)} collective-permute-done((bf16[32,4096]{1,0:T(8,128)(2,1)S(1)}, bf16[32,4096]{1,0:T(8,128)(2,1)S(1)}, u32[]{:S(2)}, u32[]{:S(2)}) %collective-permute-start.11) | collective-permute-done | bytes 262176 | tf_op jit(solution)/shard_map/ppermute | solution.py:439
  93.7 5.6 %collective-permute-done.10 = bf16[32,4096]{1,0:T(8,128)(2,1)S(1)} collective-permute-done((bf16[32,4096]{1,0:T(8,128)(2,1)S(1)}, bf16[32,4096]{1,0:T(8,128)(2,1)S(1)}, u32[]{:S(2)}, u32[]{:S(2)}) %collective-permute-start.10) | collective-permute-done | bytes 262176 | tf_op jit(solution)/shard_map/ppermute | solution.py:439
  99.3 1.1 %add_convert_fusion = bf16[32,8192]{1,0:T(8,128)(2,1)} fusion(bf16[32,8192]{1,0:T(8,128)(2,1)S(1)} %collective-permute-done.7, bf16[32,8192]{1,0:T(8,128)(2,1)S(1)} %get-tuple-element.50, bf16[32,4096]{1,0:T(8,128)(2,1)S(1)} %collective-permute-done.11, bf16[32,4096]{1,0:T(8,128)(2,1)S(1)} %collective-permute-done.10, ...), kind=kLoop, calls=%fused_computation | loop fusion | flops 3670016 | bytes 2621440 | tf_op jit(solution)/shard_map/convert_element_type | solution.py:491
  (26 shorter events, 2.0 us)
Async XLA Ops:
  50.8 4.6 %collective-permute-start = (f32[208,128]{1,0:T(8,128)S(1)}, f32[208,128]{1,0:T(8,128)S(1)}, u32[]{:S(2)}, u32[]{:S(2)}) collective-permute-start(f32[208,128]{1,0:T(8,128)S(1)} %slice_bitcast_fusion), channel_id=1, source_target_pairs={{0,32},{32,0},{1,33},{33,1},{2,34},{34,2},{3,35},{35,3},{4,36},{36... | collective-permute-start | bytes 319496 | tf_op jit(solution)/shard_map/ppermute | solution.py:435
  55.4 4.6 %collective-permute-start.3 = (f32[208,128]{1,0:T(8,128)S(1)}, f32[208,128]{1,0:T(8,128)S(1)}, u32[]{:S(2)}, u32[]{:S(2)}) collective-permute-start(f32[208,128]{1,0:T(8,128)S(1)} %bitcast_add_fusion), channel_id=1, source_target_pairs={{0,192},{64,0},{128,64},{192,128},{1,193},{65,1},{129,65},{193,129... | collective-permute-start | bytes 319496 | tf_op jit(solution)/shard_map/ppermute | solution.py:439
  58.0 7.8 %collective-permute-start.2 = (f32[208,128]{1,0:T(8,128)S(1)}, f32[208,128]{1,0:T(8,128)S(1)}, u32[]{:S(2)}, u32[]{:S(2)}) collective-permute-start(f32[208,128]{1,0:T(8,128)S(1)} %bitcast_add_fusion), channel_id=1, source_target_pairs={{0,64},{64,128},{128,192},{192,0},{1,65},{65,129},{129,193},{193,1... | collective-permute-start | bytes 319496 | tf_op jit(solution)/shard_map/ppermute | solution.py:439
  58.0 7.8 %collective-permute-start.1 = (f32[208,128]{1,0:T(8,128)S(1)}, f32[208,128]{1,0:T(8,128)S(1)}, u32[]{:S(2)}, u32[]{:S(2)}) collective-permute-start(f32[208,128]{1,0:T(8,128)S(1)} %bitcast_add_fusion), channel_id=1, source_target_pairs={{0,128},{64,192},{128,0},{192,64},{1,129},{65,193},{129,1},{193,65... | collective-permute-start | bytes 319496 | tf_op jit(solution)/shard_map/ppermute | solution.py:439
  65.8 2.1 %collective-permute-start.4 = (f32[208,128]{1,0:T(8,128)S(1)}, f32[208,128]{1,0:T(8,128)S(1)}, u32[]{:S(2)}, u32[]{:S(2)}) collective-permute-start(f32[208,128]{1,0:T(8,128)S(1)} %add_add_fusion.mine_ref), channel_id=1, source_target_pairs={{0,32},{32,0},{1,33},{33,1},{2,34},{34,2},{3,35},{35,3},{4,36},{36... | collective-permute-start | bytes 319496 | tf_op jit(solution)/shard_map/ppermute | solution.py:435
  77.6 1.6 %collective-permute-start.8 = (bf16[32,4096]{1,0:T(8,128)(2,1)S(1)}, bf16[32,4096]{1,0:T(8,128)(2,1)S(1)}, u32[]{:S(2)}, u32[]{:S(2)}) collective-permute-start(bf16[32,4096]{1,0:T(8,128)(2,1)S(1)} %get-tuple-element.53), channel_id=1, source_target_pairs={{0,32},{32,0},{1,33},{33,1},{2,34},{34,2},{3,35},{35,3},{4,36},{36... | collective-permute-start | bytes 786440 | tf_op jit(solution)/shard_map/ppermute | solution.py:435
  78.0 1.6 %collective-permute-start.13 = (bf16[32,4096]{1,0:T(8,128)(2,1)S(1)}, bf16[32,4096]{1,0:T(8,128)(2,1)S(1)}, u32[]{:S(2)}, u32[]{:S(2)}) collective-permute-start(bf16[32,4096]{1,0:T(8,128)(2,1)S(1)} %get-tuple-element.57), channel_id=1, source_target_pairs={{0,32},{32,0},{1,33},{33,1},{2,34},{34,2},{3,35},{35,3},{4,36},{36... | collective-permute-start | bytes 786440 | tf_op jit(solution)/shard_map/ppermute | solution.py:435
  78.2 4.0 %collective-permute-start.5 = (bf16[32,8192]{1,0:T(8,128)(2,1)S(1)}, bf16[32,8192]{1,0:T(8,128)(2,1)S(1)}, u32[]{:S(2)}, u32[]{:S(2)}) collective-permute-start(bf16[32,8192]{1,0:T(8,128)(2,1)S(1)} %get-tuple-element.41), channel_id=1, source_target_pairs={{0,32},{32,0},{1,33},{33,1},{2,34},{34,2},{3,35},{35,3},{4,36},{36... | collective-permute-start | bytes 1572872 | tf_op jit(solution)/shard_map/ppermute | solution.py:435
  78.5 3.7 %collective-permute-start.6 = (bf16[32,8192]{1,0:T(8,128)(2,1)S(1)}, bf16[32,8192]{1,0:T(8,128)(2,1)S(1)}, u32[]{:S(2)}, u32[]{:S(2)}) collective-permute-start(bf16[32,8192]{1,0:T(8,128)(2,1)S(1)} %get-tuple-element.42), channel_id=1, source_target_pairs={{0,32},{32,0},{1,33},{33,1},{2,34},{34,2},{3,35},{35,3},{4,36},{36... | collective-permute-start | bytes 1572872 | tf_op jit(solution)/shard_map/ppermute | solution.py:435
  78.7 13.7 %collective-permute-start.7 = (bf16[32,8192]{1,0:T(8,128)(2,1)S(1)}, bf16[32,8192]{1,0:T(8,128)(2,1)S(1)}, u32[]{:S(2)}, u32[]{:S(2)}) collective-permute-start(bf16[32,8192]{1,0:T(8,128)(2,1)S(1)} %get-tuple-element.51), channel_id=1, source_target_pairs={{0,32},{32,0},{1,33},{33,1},{2,34},{34,2},{3,35},{35,3},{4,36},{36... | collective-permute-start | bytes 1572872 | tf_op jit(solution)/shard_map/ppermute | solution.py:435
  79.3 8.8 %collective-permute-start.9 = (bf16[32,4096]{1,0:T(8,128)(2,1)S(1)}, bf16[32,4096]{1,0:T(8,128)(2,1)S(1)}, u32[]{:S(2)}, u32[]{:S(2)}) collective-permute-start(bf16[32,4096]{1,0:T(8,128)(2,1)S(1)} %add_convert_fusion.4), channel_id=1, source_target_pairs={{0,64},{64,128},{128,192},{192,0},{1,65},{65,129},{129,193},{193,1... | collective-permute-start | bytes 786440 | tf_op jit(solution)/shard_map/ppermute | solution.py:439
  79.6 8.6 %collective-permute-start.14 = (bf16[32,4096]{1,0:T(8,128)(2,1)S(1)}, bf16[32,4096]{1,0:T(8,128)(2,1)S(1)}, u32[]{:S(2)}, u32[]{:S(2)}) collective-permute-start(bf16[32,4096]{1,0:T(8,128)(2,1)S(1)} %add_convert_fusion.2), channel_id=1, source_target_pairs={{0,192},{64,0},{128,64},{192,128},{1,193},{65,1},{129,65},{193,129... | collective-permute-start | bytes 786440 | tf_op jit(solution)/shard_map/ppermute | solution.py:439
  82.3 11.4 %collective-permute-start.11 = (bf16[32,4096]{1,0:T(8,128)(2,1)S(1)}, bf16[32,4096]{1,0:T(8,128)(2,1)S(1)}, u32[]{:S(2)}, u32[]{:S(2)}) collective-permute-start(bf16[32,4096]{1,0:T(8,128)(2,1)S(1)} %add_convert_fusion.6), channel_id=1, source_target_pairs={{0,64},{64,128},{128,192},{192,0},{1,65},{65,129},{129,193},{193,1... | collective-permute-start | bytes 786440 | tf_op jit(solution)/shard_map/ppermute | solution.py:439
  82.6 11.1 %collective-permute-start.12 = (bf16[32,4096]{1,0:T(8,128)(2,1)S(1)}, bf16[32,4096]{1,0:T(8,128)(2,1)S(1)}, u32[]{:S(2)}, u32[]{:S(2)}) collective-permute-start(bf16[32,4096]{1,0:T(8,128)(2,1)S(1)} %add_convert_fusion.5), channel_id=1, source_target_pairs={{0,192},{64,0},{128,64},{192,128},{1,193},{65,1},{129,65},{193,129... | collective-permute-start | bytes 786440 | tf_op jit(solution)/shard_map/ppermute | solution.py:439
  88.2 11.1 %collective-permute-start.10 = (bf16[32,4096]{1,0:T(8,128)(2,1)S(1)}, bf16[32,4096]{1,0:T(8,128)(2,1)S(1)}, u32[]{:S(2)}, u32[]{:S(2)}) collective-permute-start(bf16[32,4096]{1,0:T(8,128)(2,1)S(1)} %add_convert_fusion.3), channel_id=1, source_target_pairs={{0,64},{64,128},{128,192},{192,0},{1,65},{65,129},{129,193},{193,1... | collective-permute-start | bytes 786440 | tf_op jit(solution)/shard_map/ppermute | solution.py:439
  88.4 10.9 %collective-permute-start.15 = (bf16[32,4096]{1,0:T(8,128)(2,1)S(1)}, bf16[32,4096]{1,0:T(8,128)(2,1)S(1)}, u32[]{:S(2)}, u32[]{:S(2)}) collective-permute-start(bf16[32,4096]{1,0:T(8,128)(2,1)S(1)} %add_convert_fusion.1), channel_id=1, source_target_pairs={{0,192},{64,0},{128,64},{192,128},{1,193},{65,1},{129,65},{193,129... | collective-permute-start | bytes 786440 | tf_op jit(solution)/shard_map/ppermute | solution.py:439
